TPU v7x, 512 devices: a whole 4x4x16 slice. The times are simulated.
512 devices in a mesh: band: 16 (over y, x_lo, core), tmpl: 32 (over z, x_hi).
Axes of the slice: x: 4 (x_hi: 2, x_lo: 2; x = x_hi * 2 + x_lo), y: 4, z: 16, core: 2. Of those that a mesh axis runs over, the one named last changes fastest.
Arguments:
- templates: float32 [2, 2048, 65536], P(None, 'tmpl', 'band'), may hold values from -100 to 100
Outputs:
- moduli: float32 [2048, 5, 64], P('tmpl')
All inputs are finite; a program needn't handle non-finite values.
Results may differ from a plain program's by a relative error of at most 0.0003.
Values sent between devices are 32-bit elements; how exact they have to be, the bound alone decides.
No kernel may reach another device: no remote copies, remote signals or barrier semaphores. Data moves between devices by JAX's collectives and lax.ppermute only.
A program may use at most 64 MiB of HBM per device.

v0:
```python
import jax
import jax.numpy as jnp
from jax import lax
from jax.sharding import PartitionSpec as P


def swapped(value, axis, distance):
    mask = 2**distance
    pairs = [(source, source ^ mask) for source in range(lax.axis_size(axis))]
    return lax.ppermute(value, axis, pairs)


def pair_tile(left_block, right_block):
    block_size = left_block.shape[1]
    left_rows = left_block.reshape(2 * block_size, left_block.shape[2])
    right_rows = right_block.reshape(2 * block_size, right_block.shape[2])
    products = lax.dot_general(
        left_rows,
        right_rows,
        (((1,), (1,)), ((), ())),
        precision=lax.Precision.HIGHEST,
        preferred_element_type=jnp.float32,
    ).reshape(2, block_size, 2, block_size)
    real_part = products[0, :, 0] + products[1, :, 1]
    imag_part = products[0, :, 1] - products[1, :, 0]
    return jnp.stack([real_part, imag_part])


def modulus(summed_tiles):
    return jnp.sqrt(summed_tiles[0] * summed_tiles[0] + summed_tiles[1] * summed_tiles[1])


def local(templates):
    energy = jnp.sum(templates * templates, axis=(0, 2))
    energy_sum = lax.psum(energy, "band")
    normed = templates / jnp.sqrt(energy_sum + 1e-06)[None, :, None]
    out_one, keep_one = (normed, normed)
    out_two, keep_two = (normed, normed)
    out_four, keep_four = (normed, normed)
    block_one = swapped(out_one, "tmpl", 0)
    block_two = swapped(out_two, "tmpl", 1)
    block_three = swapped(block_two, "tmpl", 0)
    block_four = swapped(out_four, "tmpl", 2)
    kept_blocks = (normed, keep_one, keep_two, keep_two, keep_four)
    partners = (normed, block_one, block_two, block_three, block_four)
    tiles = [pair_tile(kept, partner) for kept, partner in zip(kept_blocks, partners)]
    summed_list = []
    for tile in tiles:
        summed_list.append(lax.psum(tile, "band"))
    return modulus(jnp.stack(summed_list, axis=2))


def solution(mesh):
    in_specs = (P(None, "tmpl", "band"),)
    out_specs = P("tmpl", None, None)
    return jax.shard_map(local, mesh=mesh, in_specs=in_specs, out_specs=out_specs, check_vma=False)
```

profile of v0, /device:TPU:1, one launch (start us, length us, event | category | flops | bytes accessed | tf_op | source)
XLA Modules:
  0.0 327.7 jit_solution(14529183130818047844)
XLA Ops:
  6.5 0.0 copy-start
  6.5 0.0 all-reduce.3.cloned.1.call-start
  6.5 2.0 multiply_reduce_fusion
  8.5 33.4 %psum.42 = f32[64]{0:T(128)S(1)} all-reduce(f32[64]{0:T(128)S(1)} %multiply_reduce_fusion), channel_id=1, replica_groups=mesh['band'=16,'tmpl'=32] {'band'}, use_global_device_ids=true, to_apply=%region_1.0 | all-reduce | flops 64 | bytes 512 | tf_op jit(solution)/shard_map/psum | solution.py:35
  41.9 0.0 copy-done
  41.9 0.3 broadcast_divide_fusion
  42.2 1.9 collective-permute-start.1
  44.1 1.9 collective-permute-start.3
  46.0 3.9 %collective-permute-start = (f32[2,64,4096]{2,1,0:T(8,128)S(1)}, f32[2,64,4096]{2,1,0:T(8,128)S(1)}, u32[]{:S(2)}, u32[]{:S(2)}) collective-permute-start(f32[2,64,4096]{2,1,0:T(8,128)S(1)} %broadcast_divide_fusion), channel_id=1, source_target_pairs={{0,1},{1,0},{2,3},{3,2},{4,5},{5,4},{6,7},{7,6},{8,9},{9,8},{10,11... | collective-permute-start | bytes 6291464 | tf_op jit(solution)/shard_map/ppermute | solution.py:10
  49.9 3.1 fusion.12
  53.0 77.5 %collective-permute-done.1 = f32[2,64,4096]{2,1,0:T(8,128)S(1)} collective-permute-done((f32[2,64,4096]{2,1,0:T(8,128)S(1)}, f32[2,64,4096]{2,1,0:T(8,128)S(1)}, u32[]{:S(2)}, u32[]{:S(2)}) %collective-permute-start.1) | collective-permute-done | bytes 2097184 | tf_op jit(solution)/shard_map/ppermute | solution.py:10
  130.5 2.1 collective-permute-start.2
  132.6 5.6 %collective-permute-done.3 = f32[2,64,4096]{2,1,0:T(8,128)S(1)} collective-permute-done((f32[2,64,4096]{2,1,0:T(8,128)S(1)}, f32[2,64,4096]{2,1,0:T(8,128)S(1)}, u32[]{:S(2)}, u32[]{:S(2)}) %collective-permute-start.3) | collective-permute-done | bytes 2097184 | tf_op jit(solution)/shard_map/ppermute | solution.py:10
  138.2 3.1 fusion
  141.3 0.6 maximum_bitcast_fusion.4
  141.9 0.0 collective-permute-done
  141.9 3.1 fusion.6
  145.1 0.7 maximum_bitcast_fusion
  145.7 3.1 fusion.4
  148.8 30.7 %collective-permute-done.2 = f32[2,64,4096]{2,1,0:T(8,128)S(1)} collective-permute-done((f32[2,64,4096]{2,1,0:T(8,128)S(1)}, f32[2,64,4096]{2,1,0:T(8,128)S(1)}, u32[]{:S(2)}, u32[]{:S(2)}) %collective-permute-start.2) | collective-permute-done | bytes 2097184 | tf_op jit(solution)/shard_map/ppermute | solution.py:10
  179.5 3.1 fusion.2
  182.6 0.7 maximum_bitcast_fusion.2
  183.3 0.0 all-reduce.3.cloned.1.call-update
  183.3 132.7 %all-reduce.3.cloned.1.call-done = (f32[2,64,1,64]{3,1,0,2:T(8,128)}, f32[2,64,1,64]{3,1,0,2:T(8,128)}, f32[2,64,1,64]{3,1,0,2:T(8,128)}, f32[2,64,1,64]{3,1,0,2:T(8,128)}, f32[2,64,1,64]{3,1,0,2:T(8,128)}) async-done(((f32[2,64,1,64]{3,1,0,2:T(8,128)}, f32[2,64,1,64]{3,1,0,2:T(8,128)}, f32[2,64,1,64]{3,1,0,2:T(8,128)}, f32[2,64,1,64]{3,1,0,2:T(8,128)}, f32[2,64,1,64]{3,1,0,2:T(8,128)}), ...) | async-done | bytes 163856 | tf_op jit(solution)/shard_map/psum | solution.py:49
  316.0 0.8 constant_dynamic-update-slice_fusion.4
  316.8 0.8 constant_dynamic-update-slice_fusion.3
  317.6 0.8 constant_dynamic-update-slice_fusion.2
  318.5 0.8 constant_dynamic-update-slice_fusion.1
  319.3 0.8 constant_dynamic-update-slice_fusion
  320.2 0.7 fusion.17
  (6 shorter events, 0.1 us)
Async XLA Ops:
  6.5 35.4 %copy-start = (f32[2,64,4096]{2,1,0:T(8,128)S(1)}, f32[2,64,4096]{2,1,0:T(8,128)}, u32[]{:S(2)}) copy-start(f32[2,64,4096]{2,1,0:T(8,128)} %param.1) | copy-start | bytes 6291460
  6.5 309.4 %all-reduce.3.cloned.1.call-start = ((), (), s32[]{:S(2)}) async-start(), calls=%async_computation | async-start | bytes 655360 | tf_op jit(solution)/shard_map/psum | solution.py:49
  42.2 88.3 %collective-permute-start.1 = (f32[2,64,4096]{2,1,0:T(8,128)S(1)}, f32[2,64,4096]{2,1,0:T(8,128)S(1)}, u32[]{:S(2)}, u32[]{:S(2)}) collective-permute-start(f32[2,64,4096]{2,1,0:T(8,128)S(1)} %broadcast_divide_fusion), channel_id=1, source_target_pairs={{0,2},{1,3},{2,0},{3,1},{4,6},{5,7},{6,4},{7,5},{8,10},{9,11},{10,... | collective-permute-start | bytes 6291464 | tf_op jit(solution)/shard_map/ppermute | solution.py:10
  44.1 94.1 %collective-permute-start.3 = (f32[2,64,4096]{2,1,0:T(8,128)S(1)}, f32[2,64,4096]{2,1,0:T(8,128)S(1)}, u32[]{:S(2)}, u32[]{:S(2)}) collective-permute-start(f32[2,64,4096]{2,1,0:T(8,128)S(1)} %broadcast_divide_fusion), channel_id=1, source_target_pairs={{0,4},{1,5},{2,6},{3,7},{4,0},{5,1},{6,2},{7,3},{8,12},{9,13},{10,... | collective-permute-start | bytes 6291464 | tf_op jit(solution)/shard_map/ppermute | solution.py:10
  46.0 95.9 %collective-permute-start = (f32[2,64,4096]{2,1,0:T(8,128)S(1)}, f32[2,64,4096]{2,1,0:T(8,128)S(1)}, u32[]{:S(2)}, u32[]{:S(2)}) collective-permute-start(f32[2,64,4096]{2,1,0:T(8,128)S(1)} %broadcast_divide_fusion), channel_id=1, source_target_pairs={{0,1},{1,0},{2,3},{3,2},{4,5},{5,4},{6,7},{7,6},{8,9},{9,8},{10,11... | collective-permute-start | bytes 6291464 | tf_op jit(solution)/shard_map/ppermute | solution.py:10
  130.5 49.0 %collective-permute-start.2 = (f32[2,64,4096]{2,1,0:T(8,128)S(1)}, f32[2,64,4096]{2,1,0:T(8,128)S(1)}, u32[]{:S(2)}, u32[]{:S(2)}) collective-permute-start(f32[2,64,4096]{2,1,0:T(8,128)S(1)} %collective-permute-done.1), channel_id=1, source_target_pairs={{0,1},{1,0},{2,3},{3,2},{4,5},{5,4},{6,7},{7,6},{8,9},{9,8},{10,11... | collective-permute-start | bytes 6291464 | tf_op jit(solution)/shard_map/ppermute | solution.py:10
Sparse Core Ops, SparseCore 0:
  183.4 132.4 all-reduce.2
where the time goes:
time: 328 us
  waiting for transfers between devices  246 us (75%)
  blocking collectives  33.4 us (10%)
  matrix products  15.5 us (5%)
  between operations  13.5 us (4%)
  starting transfers between devices  9.82 us (3%)
  other arithmetic  4.97 us (2%)
  local copies, waits for them, and re-layouts  4.22 us (1%)
    psum x1, waiting for transfers between devices, local(): summed_list.append(lax.psum(tile, 'band'))  133 us
    ppermute x4, waiting for transfers between devices, swapped(): return lax.ppermute(value, axis, pairs)  114 us
    psum x1, blocking collectives, local(): energy_sum = lax.psum(energy, 'band')  33.4 us
    dot_general x5, matrix products, pair_tile(): lax.dot_general(left_rows, right_rows, (((1,), (1,)), ((), ())), precisio...  15.5 us
    ppermute x4, starting transfers between devices, swapped(): return lax.ppermute(value, axis, pairs)  9.81 us
  transfers between devices with their start and end apart: 5, of which 4 were waited for; matrix products, arithmetic and copies ran while one was open for 4% of the time, Pallas kernels for 0%

commit v1 on v0

v1 whole, which is shorter than its diff:
```python
import jax
import jax.numpy as jnp
from jax import lax
from jax.experimental import pallas as pl
from jax.experimental.pallas import tpu as pltpu
from jax.sharding import Mesh, PartitionSpec as P

BAND = ("y", "x_lo", "core")
QUAD = ("z0", "x_hi")
TMPL = ("z_hi", "z1", "z0", "x_hi")
SCALE = 2.0**30
EPSILON = 1e-06 * 2.0**60
RELAYED = True
VMEM = pl.BlockSpec(memory_space=pltpu.VMEM)


def call(kernel, shapes, *args):
    return pl.pallas_call(
        kernel,
        out_shape=shapes,
        in_specs=[VMEM] * len(args),
        out_specs=jax.tree.map(lambda _: VMEM, shapes),
        compiler_params=pltpu.CompilerParams(vmem_limit_bytes=48 * 2**20),
    )(*args)


def f32(*shape):
    return jax.ShapeDtypeStruct(shape, jnp.float32)


def split(value):
    scaled = value * SCALE
    high = scaled.astype(jnp.bfloat16)
    low = (scaled - high.astype(jnp.float32)).astype(jnp.bfloat16)
    return high, low


def dot(left, right):
    return lax.dot_general(left, right, (((1,), (1,)), ((), ())), preferred_element_type=jnp.float32)


def complex_tile(products):
    lane = lax.broadcasted_iota(jnp.int32, (64, 128), 1)
    crossed = pltpu.roll(products[64:], 64, axis=1)
    return products[:64] + jnp.where(lane < 64, crossed, -crossed)


def modulus(tile):
    real_part = jnp.abs(tile[:, :64])
    imag_part = jnp.abs(tile[:, 64:])
    large = jnp.maximum(real_part, imag_part)
    small = jnp.minimum(real_part, imag_part)
    ratio = small / jnp.where(large > 0, large, 1.0)
    return large * jnp.sqrt(1.0 + ratio * ratio)


def quad_kernel(blocks_ref, out_ref):
    rows = blocks_ref[...].reshape(512, 1024)
    high, low = split(rows)
    products = dot(high, high) + dot(high, low) + dot(low, high)
    for a in range(4):
        for k in range(4):
            b = a ^ k
            tile = complex_tile(products[128 * a : 128 * a + 128, 128 * b : 128 * b + 128])
            at = a * 16 + (k % 2) * 8
            for group in range(8):
                out_ref[2 * group + k // 2, at : at + 8, :] = tile[8 * group : 8 * group + 8]


def far_kernel(own_ref, far_ref, energy_ref, keep_ref, send_ref):
    own = jnp.concatenate(split(own_ref[...].reshape(128, 2048)), axis=0)
    far = jnp.concatenate(split(far_ref[...].reshape(128, 2048)), axis=0)
    passes = dot(own, far)
    products = passes[:128, :128] + (passes[:128, 128:] + passes[128:, :128]) + passes[128:, 128:]
    keep_ref[...] = complex_tile(products)
    send_ref[:64, :] = complex_tile(products.T)
    send_ref[64:, :] = energy_ref[...]


def pack_kernel(quad_ref, keep_ref, got_ref, out_ref):
    far_tile = keep_ref[...] + got_ref[:64, :]
    near = quad_ref[0, :16] + quad_ref[1, :16] + quad_ref[2, :16] + quad_ref[3, :16]
    near = jnp.concatenate([modulus(near[:8]), modulus(near[8:])], axis=1)
    for place in range(16):
        out_ref[place, :64, :] = far_tile
        out_ref[place, 64:72, :] = near
        for source in range(4):
            out_ref[place, 72 + source : 73 + source, :] = quad_ref[source, 16:17, :]
        out_ref[place, 76:80, :] = got_ref[64:68, :]


def final_kernel(member_ref, shares_ref, out_ref):
    member = member_ref[0]
    far_tile = shares_ref[0, :64, :]
    energies = shares_ref[0, 72:80, :]
    for place in range(1, 16):
        far_tile = far_tile + shares_ref[place, :64, :]
        energies = energies + shares_ref[place, 72:80, :]
    inverse = (1.0 / jnp.sqrt(energies + EPSILON))[:, :64]
    row = lax.broadcasted_iota(jnp.int32, (8, 64), 0)
    columns = [jnp.sum(jnp.where(row == (member ^ k), inverse, 0.0), axis=0, keepdims=True) for k in range(4)]
    columns.append(inverse[4:5])
    diagonal = lax.broadcasted_iota(jnp.int32, (64, 64), 0) == lax.broadcasted_iota(jnp.int32, (64, 64), 1)
    own = jnp.sum(jnp.where(diagonal, columns[0], 0.0), axis=1, keepdims=True)
    for k in range(5):
        if k < 4:
            at = (k % 2) * 64
            near = [shares_ref[2 * group + k // 2, 64:72, at : at + 64] for group in range(8)]
            tile = jnp.concatenate(near, axis=0)
        else:
            tile = modulus(far_tile)
        out_ref[k] = tile * own * columns[k]


def local(templates):
    z = 2 * lax.axis_index("z1") + lax.axis_index("z0")
    member = 2 * lax.axis_index("z0") + lax.axis_index("x_hi")
    own_half = lax.axis_index("z1")
    outgoing = lax.dynamic_slice_in_dim(templates, (1 - own_half) * 2048, 2048, 2)
    if RELAYED:
        passing = lax.ppermute(outgoing, ("z1", "z0"), [(1, 2), (2, 1)])
    outgoing, templates = lax.optimization_barrier((outgoing, templates))
    quarters = templates.reshape(2, 64, 4, 1024).transpose(2, 0, 1, 3)
    quad = lax.all_to_all(quarters, QUAD, 0, 0)
    if RELAYED:
        onward = jnp.where((z == 1) | (z == 2), passing, outgoing)
        far = lax.ppermute(onward, ("z1", "z0"), [(0, 2), (3, 1), (2, 3), (1, 0)])
    else:
        far = lax.ppermute(outgoing, "z1", [(0, 1), (1, 0)])
    scaled = templates * SCALE
    energy = jnp.sum(scaled * scaled, axis=(0, 2))
    energy_rows = jnp.zeros((8, 128), jnp.float32).at[0, :64].set(energy)
    own = lax.dynamic_slice_in_dim(templates, own_half * 2048, 2048, 2)

    spread = lax.all_to_all(call(quad_kernel, f32(16, 64, 128), quad), BAND, 0, 0)
    summed = jnp.sum(spread, axis=0).reshape(4, 16, 128)
    to_quad = jnp.concatenate([summed, jnp.broadcast_to(energy_rows, (4, 8, 128))], axis=1)
    from_quad = lax.all_to_all(to_quad, QUAD, 0, 0)

    keep, send = call(far_kernel, (f32(64, 128), f32(72, 128)), own, far, energy_rows)
    got = lax.ppermute(send, "z1", [(0, 1), (1, 0)])
    shares = call(pack_kernel, f32(16, 80, 128), from_quad, keep, got)
    gathered = lax.all_to_all(shares, BAND, 0, 0)
    by_offset = pl.pallas_call(
        final_kernel,
        out_shape=f32(5, 64, 64),
        in_specs=[pl.BlockSpec(memory_space=pltpu.SMEM), VMEM],
        out_specs=VMEM,
        compiler_params=pltpu.CompilerParams(vmem_limit_bytes=48 * 2**20),
    )(member.astype(jnp.int32).reshape(1), gathered)
    return by_offset.transpose(1, 0, 2)


def solution(mesh):
    devices = mesh.devices.reshape(4, 2, 2, 4, 2, 2, 2)
    finer = Mesh(devices, ("y", "x_lo", "core", "z_hi", "z1", "z0", "x_hi"))
    in_specs = (P(None, TMPL, BAND),)
    out_specs = P(TMPL, None, None)
    return jax.shard_map(local, mesh=finer, in_specs=in_specs, out_specs=out_specs, check_vma=False)
```

time: 328 us -> 95.6 us (0.29)
  waiting for transfers between devices: 246 us -> 22.4 us
  starting transfers between devices: 9.82 us -> 58.3 us
  blocking collectives: 33.4 us -> 0 us
  matrix products: 15.5 us -> 0 us
  between operations: 13.5 us -> 0.08 us
  Pallas kernels: 0 us -> 5.38 us
    psum x1 -> x0, waiting for transfers between devices: 133 us -> none  [local(): summed_list.append(lax.psum(tile, 'band'))]
    ppermute x4 -> x3, waiting for transfers between devices: 114 us -> 3.07 us  [the longest x1 3.07 us: local(): got = lax.ppermute(send, 'z1', [(0, 1), (1, 0)])]
    psum x1 -> x0, blocking collectives: 33.4 us -> none  [local(): energy_sum = lax.psum(energy, 'band')]
    all_to_all x0 -> x4, starting transfers between devices: none -> 25.2 us  [the longest x1 8.3 us: local(): lax.all_to_all(call(quad_kernel, f32(16, 64, 128), quad), BAND, 0, 0)]
    ppermute x4 -> x3, starting transfers between devices: 9.81 us -> 33.1 us  [the longest x1 28.6 us: local(): far = lax.ppermute(onward, ('z1', 'z0'), [(0, 2), (3, 1), (2, 3), (1, 0)])]
    all_to_all x0 -> x4, waiting for transfers between devices: none -> 19.3 us  [the longest x1 11.3 us: local(): gathered = lax.all_to_all(shares, BAND, 0, 0)]
    dot_general x5 -> x0, matrix products: 15.5 us -> none  [pair_tile(): lax.dot_general(left_rows, right_rows, (((1,), (1,)), ((), ())), precisio...]
    pallas_call x0 -> x4, Pallas kernels: none -> 5.38 us  [the longest x3 4.46 us: call(): pl.pallas_call(kernel, out_shape=shapes, in_specs=[VMEM] * len(args), out...]
  transfers between devices with their start and end apart: 5 -> 7, of which waited for: 4 -> 3; matrix products, arithmetic and copies ran while one was open for 4% -> 5% of each run, Pallas kernels for 0% -> 4%
where the time goes in v1:
time: 95.6 us; the launch traced here: 94.8 us
  starting transfers between devices  58.3 us (61%)
  waiting for transfers between devices  22.4 us (23%)
  Pallas kernels  5.38 us (6%)
  other arithmetic  4.7 us (5%)
  local copies, waits for them, and re-layouts  4.02 us (4%)
    ppermute x1, starting transfers between devices, local(): far = lax.ppermute(onward, ('z1', 'z0'), [(0, 2), (3, 1), (2, 3), (1, 0)])  28.6 us
    all_to_all x1, waiting for transfers between devices, local(): gathered = lax.all_to_all(shares, BAND, 0, 0)  11.3 us
    all_to_all x1, starting transfers between devices, local(): lax.all_to_all(call(quad_kernel, f32(16, 64, 128), quad), BAND, 0, 0)  8.3 us
    all_to_all x1, waiting for transfers between devices, local(): lax.all_to_all(call(quad_kernel, f32(16, 64, 128), quad), BAND, 0, 0)  7.99 us
    all_to_all x1, starting transfers between devices, local(): quad = lax.all_to_all(quarters, QUAD, 0, 0)  6.33 us
    all_to_all x1, starting transfers between devices, local(): gathered = lax.all_to_all(shares, BAND, 0, 0)  5.68 us
    all_to_all x1, starting transfers between devices, local(): from_quad = lax.all_to_all(to_quad, QUAD, 0, 0)  4.84 us
    pallas_call x3, Pallas kernels, call(): pl.pallas_call(kernel, out_shape=shapes, in_specs=[VMEM] * len(args), out...  4.46 us
  transfers between devices with their start and end apart: 7, of which 3 were waited for; matrix products, arithmetic and copies ran while one was open for 5% of the time, Pallas kernels for 4%

profile of v1, /device:TPU:1, one launch (start us, length us, event | category | flops | bytes accessed | tf_op | source)
XLA Modules:
  0.0 94.8 jit_solution(1958203685495541176)
XLA Ops:
  0.0 0.0 copy-start
  0.0 2.5 %constant_dynamic-slice_fusion.1 = f32[2,64,2048]{2,1,0:T(8,128)} fusion(f32[2,64,4096]{2,1,0:T(8,128)} %param.3, s32[]{:T(128)S(6)} %select_n.14), kind=kLoop, calls=%fused_computation.5 | loop fusion | bytes 2097156 | tf_op jit(solution)/shard_map/dynamic_slice | solution.py:119
  2.5 0.0 copy-done
  2.5 1.5 %copy.5 = f32[2,8,4,8,1024]{4,3,1,0,2:T(8,128)} copy(f32[2,8,4,8,1024]{4,3,2,1,0:T(8,128)S(1)} %bitcast.11) | data formatting | bytes 4194304 | tf_op jit(solution)/shard_map/reshape | solution.py:123
  3.9 0.0 copy-start.2
  3.9 6.3 %all-to-all-start = ((f32[4,2,64,1024]{3,2,1,0:T(8,128)}), f32[4,2,64,1024]{3,2,1,0:T(8,128)S(1)}, u32[]{:S(2)}, u32[]{:S(2)}) async-start(f32[4,2,64,1024]{3,2,1,0:T(8,128)} %bitcast.12), calls=%async_computation | async-start | bytes 4194304 | tf_op jit(solution)/shard_map/all_to_all | solution.py:124
  10.3 0.0 copy-done.2
  10.3 1.7 %collective-permute-start = (f32[2,64,2048]{2,1,0:T(8,128)S(1)}, f32[2,64,2048]{2,1,0:T(8,128)}, u32[]{:S(2)}, u32[]{:S(2)}) collective-permute-start(f32[2,64,2048]{2,1,0:T(8,128)S(1)} %copy-done.2), channel_id=1, source_target_pairs={{2,4},{4,2},{3,5},{5,3},{10,12},{12,10},{11,13},{13,11},{18,20},{2... | collective-permute-start | bytes 3145736 | tf_op jit(solution)/shard_map/ppermute | solution.py:121
  11.9 0.0 collective-permute-done
  11.9 1.1 %broadcast_select_fusion = f32[2,64,2048]{2,1,0:T(8,128)} fusion(f32[2,64,2048]{2,1,0:T(8,128)} %collective-permute-done, f32[2,64,2048]{2,1,0:T(8,128)S(1)} %copy-done.2, pred[]{:T(512)S(6)} %or.3), kind=kLoop, calls=%fused_computation.2 | loop fusion | flops 262144 | bytes 3145729 | tf_op jit(solution)/shard_map/jit(_where)/select_n | solution.py:126
  13.0 28.6 %collective-permute-start.1 = (f32[2,64,2048]{2,1,0:T(8,128)}, f32[2,64,2048]{2,1,0:T(8,128)S(1)}, u32[]{:S(2)}, u32[]{:S(2)}) collective-permute-start(f32[2,64,2048]{2,1,0:T(8,128)} %broadcast_select_fusion), channel_id=1, source_target_pairs={{0,4},{6,2},{4,6},{2,0},{1,5},{7,3},{5,7},{3,1},{8,12},{14,10},{12... | collective-permute-start | bytes 3145736 | tf_op jit(solution)/shard_map/ppermute | solution.py:127
  41.7 0.0 all-to-all-done.blocks_ref
  41.7 2.7 %shard_map.17 = f32[16,64,128]{2,1,0:T(8,128)} custom-call(f32[4,2,64,1024]{3,2,1,0:T(8,128)S(1)} %all-to-all-done.blocks_ref), custom_call_target="tpu_custom_call" | custom-call | tf_op jit(solution)/shard_map/pallas_call | solution.py:18
  44.4 0.0 copy-start.1
  44.4 8.3 %all-to-all-start.1 = ((f32[16,64,128]{2,1,0:T(8,128)}), f32[16,64,128]{2,1,0:T(8,128)}, u32[]{:S(2)}, u32[]{:S(2)}) async-start(f32[16,64,128]{2,1,0:T(8,128)} %shard_map.17), calls=%async_computation.1 | async-start | bytes 1048576 | tf_op jit(solution)/shard_map/all_to_all | solution.py:135
  52.7 1.9 %multiply_reduce_fusion = f32[64]{0:T(128)S(1)} fusion(f32[2,64,4096]{2,1,0:T(8,128)} %param.3), kind=kLoop, calls=%fused_computation.1 | loop fusion | flops 1572800 | bytes 2097408 | tf_op jit(solution)/shard_map/reduce_sum | solution.py:131
  54.6 8.0 %all-to-all-done.1 = f32[16,64,128]{2,1,0:T(8,128)} async-done(((f32[16,64,128]{2,1,0:T(8,128)}), f32[16,64,128]{2,1,0:T(8,128)}, u32[]{:S(2)}, u32[]{:S(2)}) %all-to-all-start.1) | async-done | bytes 524320 | tf_op jit(solution)/shard_map/all_to_all | solution.py:135
  62.6 1.1 %reduce_sum.18 = f32[64,128]{1,0:T(8,128)S(1)} reduce(f32[16,64,128]{2,1,0:T(8,128)} %all-to-all-done.1, f32[]{:T(128)} %constant.48.clone.1), dimensions={0}, to_apply=%region_0.1 | reduce | flops 122880 | bytes 557060 | tf_op jit(solution)/shard_map/reduce_sum | solution.py:136
  63.7 0.6 pad_maximum_fusion
  64.3 4.8 %all-to-all-start.2 = ((f32[4,24,128]{2,1,0:T(8,128)}), f32[4,24,128]{2,1,0:T(8,128)S(1)}, u32[]{:S(2)}, u32[]{:S(2)}) async-start(f32[4,24,128]{2,1,0:T(8,128)} %pad_maximum_fusion), calls=%async_computation.2 | async-start | bytes 98304 | tf_op jit(solution)/shard_map/all_to_all | solution.py:138
  69.2 0.0 copy-done.1
  69.2 0.1 constant_dynamic-slice_fusion.own_ref
  69.2 0.0 collective-permute-done.1.far_ref
  69.2 0.7 shard_map.18
  70.0 2.8 %collective-permute-start.2 = (f32[72,128]{1,0:T(8,128)S(1)}, f32[72,128]{1,0:T(8,128)S(1)}, u32[]{:S(2)}, u32[]{:S(2)}) collective-permute-start(f32[72,128]{1,0:T(8,128)S(1)} %get-tuple-element.24), channel_id=1, source_target_pairs={{0,4},{4,0},{1,5},{5,1},{2,6},{6,2},{3,7},{7,3},{8,12},{12,8},{9,1... | collective-permute-start | bytes 110600 | tf_op jit(solution)/shard_map/ppermute | solution.py:141
  72.8 3.1 %collective-permute-done.2.got_ref = f32[72,128]{1,0:T(8,128)S(1)} collective-permute-done((f32[72,128]{1,0:T(8,128)S(1)}, f32[72,128]{1,0:T(8,128)S(1)}, u32[]{:S(2)}, u32[]{:S(2)}) %collective-permute-start.2) | collective-permute-done | bytes 36896 | tf_op jit(solution)/shard_map/ppermute | solution.py:141
  75.9 0.0 all-to-all-done.2.quad_ref
  75.9 1.0 %shard_map.19 = f32[16,80,128]{2,1,0:T(8,128)} custom-call(f32[4,24,128]{2,1,0:T(8,128)S(1)} %all-to-all-done.2.quad_ref, f32[64,128]{1,0:T(8,128)S(1)} %get-tuple-element.23.keep_ref, f32[72,128]{1,0:T(8,128)S(1)} %collective-permute-done.2.got_ref), custom_call_target="tpu_custom_call" | custom-call | tf_op jit(solution)/shard_map/pallas_call | solution.py:18
  76.9 5.7 %all-to-all-start.3 = ((f32[16,80,128]{2,1,0:T(8,128)}), f32[16,80,128]{2,1,0:T(8,128)S(1)}, u32[]{:S(2)}, u32[]{:S(2)}) async-start(f32[16,80,128]{2,1,0:T(8,128)} %shard_map.19), calls=%async_computation.3 | async-start | bytes 1310720 | tf_op jit(solution)/shard_map/all_to_all | solution.py:143
  82.6 11.3 %all-to-all-done.3.shares_ref = f32[16,80,128]{2,1,0:T(8,128)S(1)} async-done(((f32[16,80,128]{2,1,0:T(8,128)}), f32[16,80,128]{2,1,0:T(8,128)S(1)}, u32[]{:S(2)}, u32[]{:S(2)}) %all-to-all-start.3) | async-done | bytes 655392 | tf_op jit(solution)/shard_map/all_to_all | solution.py:143
  93.9 0.9 shard_map.20
  (2 shorter events, 0.0 us)
Async XLA Ops:
  0.0 2.5 %copy-start = (f32[2,64,4096]{2,1,0:T(8,128)S(1)}, f32[2,64,4096]{2,1,0:T(8,128)}, u32[]{:S(2)}) copy-start(f32[2,64,4096]{2,1,0:T(8,128)} %param.3) | copy-start | bytes 6291460
  3.9 6.3 %copy-start.2 = (f32[2,64,2048]{2,1,0:T(8,128)S(1)}, f32[2,64,2048]{2,1,0:T(8,128)}, u32[]{:S(2)}) copy-start(f32[2,64,2048]{2,1,0:T(8,128)} %constant_dynamic-slice_fusion.1) | copy-start | bytes 3145732
  3.9 37.7 %all-to-all-start = ((f32[4,2,64,1024]{3,2,1,0:T(8,128)}), f32[4,2,64,1024]{3,2,1,0:T(8,128)S(1)}, u32[]{:S(2)}, u32[]{:S(2)}) async-start(f32[4,2,64,1024]{3,2,1,0:T(8,128)} %bitcast.12), calls=%async_computation | async-start | bytes 4194304 | tf_op jit(solution)/shard_map/all_to_all | solution.py:124
  10.3 1.7 %collective-permute-start = (f32[2,64,2048]{2,1,0:T(8,128)S(1)}, f32[2,64,2048]{2,1,0:T(8,128)}, u32[]{:S(2)}, u32[]{:S(2)}) collective-permute-start(f32[2,64,2048]{2,1,0:T(8,128)S(1)} %copy-done.2), channel_id=1, source_target_pairs={{2,4},{4,2},{3,5},{5,3},{10,12},{12,10},{11,13},{13,11},{18,20},{2... | collective-permute-start | bytes 3145736 | tf_op jit(solution)/shard_map/ppermute | solution.py:121
  13.0 56.2 %collective-permute-start.1 = (f32[2,64,2048]{2,1,0:T(8,128)}, f32[2,64,2048]{2,1,0:T(8,128)S(1)}, u32[]{:S(2)}, u32[]{:S(2)}) collective-permute-start(f32[2,64,2048]{2,1,0:T(8,128)} %broadcast_select_fusion), channel_id=1, source_target_pairs={{0,4},{6,2},{4,6},{2,0},{1,5},{7,3},{5,7},{3,1},{8,12},{14,10},{12... | collective-permute-start | bytes 3145736 | tf_op jit(solution)/shard_map/ppermute | solution.py:127
  44.4 24.8 %copy-start.1 = (f32[2,64,4096]{2,1,0:T(8,128)S(1)}, f32[2,64,4096]{2,1,0:T(8,128)}, u32[]{:S(2)}) copy-start(f32[2,64,4096]{2,1,0:T(8,128)} %param.3) | copy-start | bytes 6291460
  44.4 18.2 %all-to-all-start.1 = ((f32[16,64,128]{2,1,0:T(8,128)}), f32[16,64,128]{2,1,0:T(8,128)}, u32[]{:S(2)}, u32[]{:S(2)}) async-start(f32[16,64,128]{2,1,0:T(8,128)} %shard_map.17), calls=%async_computation.1 | async-start | bytes 1048576 | tf_op jit(solution)/shard_map/all_to_all | solution.py:135
  64.3 11.6 %all-to-all-start.2 = ((f32[4,24,128]{2,1,0:T(8,128)}), f32[4,24,128]{2,1,0:T(8,128)S(1)}, u32[]{:S(2)}, u32[]{:S(2)}) async-start(f32[4,24,128]{2,1,0:T(8,128)} %pad_maximum_fusion), calls=%async_computation.2 | async-start | bytes 98304 | tf_op jit(solution)/shard_map/all_to_all | solution.py:138
  70.0 5.9 %collective-permute-start.2 = (f32[72,128]{1,0:T(8,128)S(1)}, f32[72,128]{1,0:T(8,128)S(1)}, u32[]{:S(2)}, u32[]{:S(2)}) collective-permute-start(f32[72,128]{1,0:T(8,128)S(1)} %get-tuple-element.24), channel_id=1, source_target_pairs={{0,4},{4,0},{1,5},{5,1},{2,6},{6,2},{3,7},{7,3},{8,12},{12,8},{9,1... | collective-permute-start | bytes 110600 | tf_op jit(solution)/shard_map/ppermute | solution.py:141
  76.9 17.0 %all-to-all-start.3 = ((f32[16,80,128]{2,1,0:T(8,128)}), f32[16,80,128]{2,1,0:T(8,128)S(1)}, u32[]{:S(2)}, u32[]{:S(2)}) async-start(f32[16,80,128]{2,1,0:T(8,128)} %shard_map.19), calls=%async_computation.3 | async-start | bytes 1310720 | tf_op jit(solution)/shard_map/all_to_all | solution.py:143

commit v2 on v1

v2 whole, which is shorter than its diff:
```python
import functools

import jax
import jax.numpy as jnp
from jax import lax
from jax.experimental import pallas as pl
from jax.experimental.pallas import tpu as pltpu
from jax.sharding import Mesh, PartitionSpec as P

BAND = ("y", "x_lo", "core")
QUAD = ("z0", "x_hi")
FAR = ("z1", "x_lo", "core")
TMPL = ("z_hi", "z1", "z0", "x_hi")
SCALE = 2.0**30
EPSILON = 1e-06 * 2.0**60
VMEM = pl.BlockSpec(memory_space=pltpu.VMEM)
HBM = pl.BlockSpec(memory_space=pltpu.HBM)


def call(kernel, shapes, *args):
    return pl.pallas_call(
        kernel,
        out_shape=shapes,
        in_specs=[VMEM] * len(args),
        out_specs=jax.tree.map(lambda _: VMEM, shapes),
        compiler_params=pltpu.CompilerParams(vmem_limit_bytes=16 * 2**20),
    )(*args)


def f32(*shape):
    return jax.ShapeDtypeStruct(shape, jnp.float32)


def split(value):
    scaled = value * SCALE
    high = scaled.astype(jnp.bfloat16)
    low = (scaled - high.astype(jnp.float32)).astype(jnp.bfloat16)
    return high, low


def dot(left, right):
    return lax.dot_general(left, right, (((1,), (1,)), ((), ())), preferred_element_type=jnp.float32)


def complex_tile(products):
    lane = lax.broadcasted_iota(jnp.int32, (64, 128), 1)
    crossed = pltpu.roll(products[64:], 64, axis=1)
    return products[:64] + jnp.where(lane < 64, crossed, -crossed)


def modulus(tile):
    real_part = jnp.abs(tile[:, :64])
    imag_part = jnp.abs(tile[:, 64:])
    large = jnp.maximum(real_part, imag_part)
    small = jnp.minimum(real_part, imag_part)
    ratio = small / jnp.where(large > 0, large, 1.0)
    return large * jnp.sqrt(1.0 + ratio * ratio)


def member_index():
    return 2 * lax.axis_index("z0") + lax.axis_index("x_hi")


def is_middle():
    return lax.axis_index("z1") != lax.axis_index("z0")


def half_kernel(at, templates_ref, out_ref, sem):
    copy = pltpu.make_async_copy(templates_ref.at[:, :, at : at + 2048], out_ref, sem)
    copy.start()
    copy.wait()


def half(templates, at):
    return pl.pallas_call(
        functools.partial(half_kernel, at),
        out_shape=f32(2, 64, 2048),
        in_specs=[HBM],
        out_specs=VMEM,
        scratch_shapes=[pltpu.SemaphoreType.DMA],
        compiler_params=pltpu.CompilerParams(vmem_limit_bytes=8 * 2**20),
    )(templates)


def quarters_kernel(offsets, templates_ref, *refs):
    copies = []
    for place, offset in enumerate(offsets):
        at = pl.multiple_of((member_index() ^ offset) * 1024, 1024)
        copies.append(pltpu.make_async_copy(templates_ref.at[:, :, pl.ds(at, 1024)], refs[place], refs[-1].at[place]))
    for copy in copies:
        copy.start()
    for copy in copies:
        copy.wait()


def quarters(templates, *offsets):
    return pl.pallas_call(
        functools.partial(quarters_kernel, offsets),
        out_shape=(f32(2, 64, 1024),) * len(offsets),
        in_specs=[HBM],
        out_specs=(VMEM,) * len(offsets),
        scratch_shapes=[pltpu.SemaphoreType.DMA((len(offsets),))],
        compiler_params=pltpu.CompilerParams(vmem_limit_bytes=8 * 2**20),
    )(templates)


def choose_kernel(second_ref, passing_ref, out_ref, sem):
    @pl.when(is_middle())
    def _():
        copy = pltpu.make_async_copy(passing_ref, out_ref, sem)
        copy.start()
        copy.wait()

    @pl.when(jnp.logical_not(is_middle()))
    def _():
        copy = pltpu.make_async_copy(second_ref, out_ref, sem)
        copy.start()
        copy.wait()


def choose(second, passing):
    return pl.pallas_call(
        choose_kernel,
        out_shape=f32(2, 64, 2048),
        in_specs=[VMEM] * 2,
        out_specs=VMEM,
        scratch_shapes=[pltpu.SemaphoreType.DMA],
        compiler_params=pltpu.CompilerParams(vmem_limit_bytes=8 * 2**20),
    )(second, passing)


def row_of(column):
    row = lax.broadcasted_iota(jnp.int32, (64, 128), 0)
    lane = lax.broadcasted_iota(jnp.int32, (64, 128), 1)
    return jnp.sum(jnp.where(row == lane, column, 0.0), axis=0, keepdims=True)


def own_kernel(templates_ref, own_ref, energy_ref):
    at = pl.multiple_of(jnp.where(is_middle(), 2048, 0), 2048)
    high, low = split(templates_ref[:, :, pl.ds(at, 2048)].reshape(128, 2048))
    own_ref[:128, :] = high
    own_ref[128:, :] = low
    squares = jnp.zeros((64, 128), jnp.float32)
    for start in range(0, 4096, 128):
        for part in range(2):
            values = templates_ref[part, :, start : start + 128] * SCALE
            squares = squares + values * values
    energy_ref[...] = jnp.zeros((8, 128), jnp.float32)
    energy_ref[:1, :] = row_of(jnp.sum(squares, axis=1, keepdims=True))


def near_kernel(own_ref, three_ref, two_ref, one_ref, out_ref):
    blocks = [own_ref[...], one_ref[...], two_ref[...], three_ref[...]]
    rows = jnp.concatenate([block.reshape(128, 1024) for block in blocks], axis=0)
    high, low = split(rows)
    products = dot(high, high) + dot(high, low) + dot(low, high)
    row = lax.broadcasted_iota(jnp.int32, (64, 128), 0)
    lane = lax.broadcasted_iota(jnp.int32, (64, 128), 1)
    energies = []
    for a in range(4):
        for k in range(4):
            b = a ^ k
            tile = complex_tile(products[128 * a : 128 * a + 128, 128 * b : 128 * b + 128])
            if k == 0:
                energies.append(jnp.sum(jnp.where(row == lane, tile, 0.0), axis=0, keepdims=True))
            at = 16 * a + 8 * (k % 2)
            for group in range(8):
                out_ref[2 * group + k // 2, at : at + 8, :] = tile[8 * group : 8 * group + 8]
    energies = jnp.concatenate(energies + [jnp.zeros((4, 128), jnp.float32)], axis=0)
    for place in range(16):
        out_ref[place, 64:, :] = energies


def sum_kernel(spread_ref, out_ref):
    total = spread_ref[0]
    for place in range(1, 16):
        total = total + spread_ref[place]
    for offset in range(4):
        to = member_index() ^ offset
        out_ref[to, :16, :] = total[16 * offset : 16 * offset + 16]
        for k in range(4):
            out_ref[to, 16 + k : 17 + k, :] = total[64 + (offset ^ k) : 65 + (offset ^ k)]
        out_ref[to, 20:, :] = jnp.zeros((4, 128), jnp.float32)


def far_kernel(own_ref, energy_ref, far_ref, out_ref):
    side = lax.axis_index("z1")
    passes = dot(own_ref[...], jnp.concatenate(split(far_ref[...].reshape(128, 2048)), axis=0))
    products = passes[:128, :128] + (passes[:128, 128:] + passes[128:, :128]) + passes[128:, 128:]
    here = complex_tile(products)
    there = complex_tile(products.T)
    for quarter in range(4):
        same = 4 * side + quarter
        other = 4 * (1 - side) + quarter
        out_ref[same, :16, :] = here[16 * quarter : 16 * quarter + 16]
        out_ref[other, :16, :] = there[16 * quarter : 16 * quarter + 16]
        out_ref[same, 16:, :] = jnp.zeros((8, 128), jnp.float32)
        out_ref[other, 16:, :] = energy_ref[...]


def pack_kernel(near_ref, far_ref, out_ref):
    far = far_ref[0]
    for place in range(1, 8):
        far = far + far_ref[place]
    near = near_ref[0, :16, :] + near_ref[1, :16, :] + near_ref[2, :16, :] + near_ref[3, :16, :]
    near = jnp.concatenate([modulus(near[:8]), modulus(near[8:])], axis=1)
    for place in range(16):
        out_ref[place, :16, :] = far[:16]
        out_ref[place, 16:24, :] = near
        out_ref[place, 24:, :] = far[16:]


def final_kernel(near_ref, shares_ref, out_ref):
    energies = near_ref[0, 16:, :64] + near_ref[1, 16:, :64] + near_ref[2, 16:, :64] + near_ref[3, 16:, :64]
    far_energies = shares_ref[0, 24:, :64]
    for place in range(1, 16):
        far_energies = far_energies + shares_ref[place, 24:, :64]
    inverse = 1.0 / jnp.sqrt(energies + EPSILON)
    far_inverse = 1.0 / jnp.sqrt(far_energies * 0.25 + EPSILON)
    columns = [inverse[k : k + 1] for k in range(4)] + [far_inverse[:1]]
    diagonal = lax.broadcasted_iota(jnp.int32, (64, 64), 0) == lax.broadcasted_iota(jnp.int32, (64, 64), 1)
    rows = jnp.sum(jnp.where(diagonal, columns[0], 0.0), axis=1, keepdims=True)
    for k in range(5):
        if k < 4:
            at = 64 * (k % 2)
            tile = [shares_ref[2 * group + k // 2, 16:24, at : at + 64] for group in range(8)]
            tile = jnp.concatenate(tile, axis=0)
        else:
            far = [sum(shares_ref[4 * y + quarter, :16, :] for y in range(4)) for quarter in range(4)]
            tile = modulus(jnp.concatenate(far, axis=0))
        out_ref[k] = tile * rows * columns[k]


def swapped(value, offset):
    pairs = [(source, source ^ offset) for source in range(4)]
    return lax.ppermute(value, QUAD, pairs)


def local(templates):
    templates = pltpu.with_memory_space_constraint(templates, pltpu.HBM)
    (quarter,) = quarters(templates, 3)
    three = swapped(quarter, 3)
    quarter, templates = lax.optimization_barrier((quarter, templates))
    first = half(templates, 0)
    passing = lax.ppermute(first, ("z1", "z0"), [(1, 2), (2, 1)])
    first, templates = lax.optimization_barrier((first, templates))
    mine, other, quarter = quarters(templates, 0, 1, 2)
    two = swapped(quarter, 2)
    one = swapped(other, 1)
    blocks = [mine, three, two, one]
    own, energy = call(own_kernel, (jax.ShapeDtypeStruct((256, 2048), jnp.bfloat16), f32(8, 128)), templates)
    second = half(templates, 2048)
    second, passing, own = lax.optimization_barrier((second, passing, own))
    onward = lax.ppermute(choose(second, passing), ("z1", "z0"), [(0, 2), (3, 1), (2, 3), (1, 0)])

    blocks, own = lax.optimization_barrier((blocks, own))
    spread = lax.all_to_all(call(near_kernel, f32(16, 72, 128), *blocks), BAND, 0, 0)
    near = lax.all_to_all(call(sum_kernel, f32(4, 24, 128), spread), QUAD, 0, 0)
    near, own = lax.optimization_barrier((near, own))
    far = lax.all_to_all(call(far_kernel, f32(8, 24, 128), own, energy, onward), FAR, 0, 0)
    shares = lax.all_to_all(call(pack_kernel, f32(16, 32, 128), near, far), BAND, 0, 0)
    return call(final_kernel, f32(5, 64, 64), near, shares).transpose(1, 0, 2)


def solution(mesh):
    devices = mesh.devices.reshape(4, 2, 2, 4, 2, 2, 2)
    finer = Mesh(devices, ("y", "x_lo", "core", "z_hi", "z1", "z0", "x_hi"))
    in_specs = (P(None, TMPL, BAND),)
    out_specs = P(TMPL, None, None)
    return jax.shard_map(local, mesh=finer, in_specs=in_specs, out_specs=out_specs, check_vma=False)
```

time: 95.6 us -> 88 us (0.921)
  blocking collectives: 0 us -> 48.1 us
  starting transfers between devices: 58.3 us -> 26.7 us
  waiting for transfers between devices: 22.4 us -> 1.67 us
  Pallas kernels: 5.38 us -> 10.8 us
  other arithmetic: 4.7 us -> 0 us
  local copies, waits for them, and re-layouts: 4.02 us -> 0 us
    all_to_all x0 -> x4, blocking collectives: none -> 48.1 us  [the longest x1 17 us: local(): lax.all_to_all(call(near_kernel, f32(16, 72, 128), *blocks), BAND, 0, 0)]
    all_to_all x4 -> x0, starting transfers between devices: 25.2 us -> none  [the longest x1 8.3 us: local(): lax.all_to_all(call(quad_kernel, f32(16, 64, 128), quad), BAND, 0, 0)]
    all_to_all x4 -> x0, waiting for transfers between devices: 19.3 us -> none  [the longest x1 11.3 us: local(): gathered = lax.all_to_all(shares, BAND, 0, 0)]
    ppermute x3 -> x5, starting transfers between devices: 33.1 us -> 26.7 us  [the longest x3 13.8 us: swapped(): return lax.ppermute(value, QUAD, pairs)]
    pallas_call x1 -> x5, Pallas kernels: 0.92 us -> 5.02 us  [the longest x2 2.47 us: half(): pl.pallas_call(functools.partial(half_kernel, at), out_shape=f32(2, 64, 2...]
    reduce_sum x2 -> x0, other arithmetic: 2.97 us -> none  [the longest x1 1.89 us: local(): energy = jnp.sum(scaled * scaled, axis=(0, 2))]
    dynamic_slice x2 -> x0, local copies, waits for them, and re-layouts: 2.52 us -> none  [the longest x1 2.45 us: local(): lax.dynamic_slice_in_dim(templates, (1 - own_half) * 2048, 2048, 2)]
    reshape x1 -> x0, local copies, waits for them, and re-layouts: 1.48 us -> none  [local(): quarters = templates.reshape(2, 64, 4, 1024).transpose(2, 0, 1, 3)]
  transfers between devices with their start and end apart: 7 -> 5, of which waited for: 3 -> 2; matrix products, arithmetic and copies ran while one was open for 5% -> 0% of each run, Pallas kernels for 4% -> 8%
where the time goes in v2:
time: 88 us; the launch traced here: 87.5 us
  blocking collectives  48.1 us (55%)
  starting transfers between devices  26.7 us (30%)
  Pallas kernels  10.8 us (12%)
  waiting for transfers between devices  1.67 us (2%)
    all_to_all x1, blocking collectives, local(): lax.all_to_all(call(near_kernel, f32(16, 72, 128), *blocks), BAND, 0, 0)  17 us
    ppermute x3, starting transfers between devices, swapped(): return lax.ppermute(value, QUAD, pairs)  13.8 us
    ppermute x1, starting transfers between devices, local(): lax.ppermute(choose(second, passing), ('z1', 'z0'), [(0, 2), (3, 1), (2,...  12.3 us
    all_to_all x1, blocking collectives, local(): lax.all_to_all(call(far_kernel, f32(8, 24, 128), own, energy, onward), FA...  10.4 us
    all_to_all x1, blocking collectives, local(): lax.all_to_all(call(pack_kernel, f32(16, 32, 128), near, far), BAND, 0, 0)  10.4 us
    all_to_all x1, blocking collectives, local(): near = lax.all_to_all(call(sum_kernel, f32(4, 24, 128), spread), QUAD, 0, 0)  10.3 us
    pallas_call x6, Pallas kernels, call(): pl.pallas_call(kernel, out_shape=shapes, in_specs=[VMEM] * len(args), out...  5.79 us
    pallas_call x2, Pallas kernels, half(): pl.pallas_call(functools.partial(half_kernel, at), out_shape=f32(2, 64, 2...  2.47 us
  transfers between devices with their start and end apart: 5, of which 2 were waited for; matrix products, arithmetic and copies ran while one was open for 0% of the time, Pallas kernels for 8%

profile of v2, /device:TPU:1, one launch (start us, length us, event | category | flops | bytes accessed | tf_op | source)
XLA Modules:
  0.0 87.5 jit_solution(13239801955431924794)
XLA Ops:
  0.0 1.0 %shard_map.17 = f32[2,64,1024]{2,1,0:T(8,128)S(1)} custom-call(f32[2,64,4096]{2,1,0:T(8,128)} %templates_ref.5), custom_call_target="tpu_custom_call" | custom-call | tf_op jit(solution)/shard_map/pallas_call | solution.py:97
  1.1 1.2 %shard_map.18 = f32[2,64,2048]{2,1,0:T(8,128)S(1)} custom-call(f32[2,64,4096]{2,1,0:T(8,128)} %templates_ref.5), custom_call_target="tpu_custom_call" | custom-call | tf_op jit(solution)/shard_map/pallas_call | solution.py:75
  2.3 0.7 collective-permute-start.3
  3.0 9.7 %collective-permute-start = (f32[2,64,1024]{2,1,0:T(8,128)S(1)}, f32[2,64,1024]{2,1,0:T(8,128)S(1)}, u32[]{:S(2)}, u32[]{:S(2)}) collective-permute-start(f32[2,64,1024]{2,1,0:T(8,128)S(1)} %shard_map.17), channel_id=1, source_target_pairs={{0,3},{1,2},{2,1},{3,0},{4,7},{5,6},{6,5},{7,4},{8,11},{9,10},{10,... | collective-permute-start | bytes 1572872 | tf_op jit(solution)/shard_map/ppermute | solution.py:236
  12.7 1.4 %shard_map.19 = (f32[2,64,1024]{2,1,0:T(8,128)S(1)}, f32[2,64,1024]{2,1,0:T(8,128)S(1)}, f32[2,64,1024]{2,1,0:T(8,128)S(1)}) custom-call(f32[2,64,4096]{2,1,0:T(8,128)} %templates_ref.5), custom_call_target="tpu_custom_call" | custom-call | tf_op jit(solution)/shard_map/pallas_call | solution.py:97
  14.1 1.9 %collective-permute-start.1 = (f32[2,64,1024]{2,1,0:T(8,128)S(1)}, f32[2,64,1024]{2,1,0:T(8,128)S(1)}, u32[]{:S(2)}, u32[]{:S(2)}) collective-permute-start(f32[2,64,1024]{2,1,0:T(8,128)S(1)} %get-tuple-element.25), channel_id=1, source_target_pairs={{0,2},{1,3},{2,0},{3,1},{4,6},{5,7},{6,4},{7,5},{8,10},{9,11},{10,... | collective-permute-start | bytes 1572872 | tf_op jit(solution)/shard_map/ppermute | solution.py:236
  16.0 2.2 %collective-permute-start.2 = (f32[2,64,1024]{2,1,0:T(8,128)S(1)}, f32[2,64,1024]{2,1,0:T(8,128)S(1)}, u32[]{:S(2)}, u32[]{:S(2)}) collective-permute-start(f32[2,64,1024]{2,1,0:T(8,128)S(1)} %get-tuple-element.26), channel_id=1, source_target_pairs={{0,1},{1,0},{2,3},{3,2},{4,5},{5,4},{6,7},{7,6},{8,9},{9,8},{10,11... | collective-permute-start | bytes 1572872 | tf_op jit(solution)/shard_map/ppermute | solution.py:236
  18.2 1.2 %shard_map.20.second_ref = f32[2,64,2048]{2,1,0:T(8,128)S(1)} custom-call(f32[2,64,4096]{2,1,0:T(8,128)} %templates_ref.5), custom_call_target="tpu_custom_call" | custom-call | tf_op jit(solution)/shard_map/pallas_call | solution.py:75
  19.5 2.2 %shard_map.21 = (bf16[256,2048]{1,0:T(8,128)(2,1)S(1)}, f32[8,128]{1,0:T(8,128)S(1)}) custom-call(f32[2,64,4096]{2,1,0:T(8,128)} %templates_ref.5), custom_call_target="tpu_custom_call" | custom-call | tf_op jit(solution)/shard_map/pallas_call | solution.py:21
  21.7 0.0 collective-permute-done.3.passing_ref
  21.7 0.1 shard_map.24
  21.8 12.3 %collective-permute-start.4 = (f32[2,64,2048]{2,1,0:T(8,128)S(1)}, f32[2,64,2048]{2,1,0:T(8,128)S(1)}, u32[]{:S(2)}, u32[]{:S(2)}) collective-permute-start(f32[2,64,2048]{2,1,0:T(8,128)S(1)} %shard_map.24), channel_id=1, source_target_pairs={{0,4},{6,2},{4,6},{2,0},{1,5},{7,3},{5,7},{3,1},{8,12},{14,10},{12... | collective-permute-start | bytes 3145736 | tf_op jit(solution)/shard_map/ppermute | solution.py:254
  34.0 0.0 collective-permute-done.three_ref
  34.1 0.2 collective-permute-done.1.two_ref
  34.2 1.5 %collective-permute-done.2.one_ref = f32[2,64,1024]{2,1,0:T(8,128)S(1)} collective-permute-done((f32[2,64,1024]{2,1,0:T(8,128)S(1)}, f32[2,64,1024]{2,1,0:T(8,128)S(1)}, u32[]{:S(2)}, u32[]{:S(2)}) %collective-permute-start.2) | collective-permute-done | bytes 524320 | tf_op jit(solution)/shard_map/ppermute | solution.py:236
  35.7 1.9 %shard_map.22 = f32[16,72,128]{2,1,0:T(8,128)S(1)} custom-call(f32[2,64,1024]{2,1,0:T(8,128)S(1)} %get-tuple-element.29.own_ref, f32[2,64,1024]{2,1,0:T(8,128)S(1)} %collective-permute-done.three_ref, f32[2,64,1024]{2,1,0:T(8,128)S(1)} %collective-permute-done.1.two_ref, f32[2,64,1024]{2,1,0:T(8,128)S(1)} %collective-permute-done.2.one_ref), custom_call_target="tpu_custom_call" | custom-call | tf_op jit(solution)/shard_map/pallas_call | solution.py:21
  37.7 17.0 %all_to_all.20.spread_ref = f32[16,72,128]{2,1,0:T(8,128)S(1)} all-to-all(f32[16,72,128]{2,1,0:T(8,128)S(1)} %shard_map.22), channel_id=1, replica_groups=mesh['y'=4,'x_lo'=2,'core'=2,'z_hi'=4,'z1'=2,'z0'=2,'x_hi'=2] {'y','x_lo..., dimensions={0} | all-to-all | bytes 1179648 | tf_op jit(solution)/shard_map/all_to_all | solution.py:257
  54.7 10.3 %all_to_all.21.near_ref = f32[4,24,128]{2,1,0:T(8,128)S(1)} all-to-all(f32[4,24,128]{2,1,0:T(8,128)S(1)} %shard_map.23), channel_id=1, replica_groups=mesh['y'=4,'x_lo'=2,'core'=2,'z_hi'=4,'z1'=2,'z0'=2,'x_hi'=2] {'z0','x_hi'}, dimensions={0} | all-to-all | bytes 98304 | tf_op jit(solution)/shard_map/all_to_all | solution.py:258
  65.0 0.0 collective-permute-done.4.far_ref
  65.0 0.6 shard_map.25
  65.6 10.4 %all_to_all.22.far_ref = f32[8,24,128]{2,1,0:T(8,128)S(1)} all-to-all(f32[8,24,128]{2,1,0:T(8,128)S(1)} %shard_map.25), channel_id=1, replica_groups=mesh['y'=4,'x_lo'=2,'core'=2,'z_hi'=4,'z1'=2,'z0'=2,'x_hi'=2] {'z1','x_l..., dimensions={0} | all-to-all | bytes 196608 | tf_op jit(solution)/shard_map/all_to_all | solution.py:260
  76.1 0.2 shard_map.26
  76.2 10.4 %all_to_all.23.shares_ref = f32[16,32,128]{2,1,0:T(8,128)S(1)} all-to-all(f32[16,32,128]{2,1,0:T(8,128)S(1)} %shard_map.26), channel_id=1, replica_groups=mesh['y'=4,'x_lo'=2,'core'=2,'z_hi'=4,'z1'=2,'z0'=2,'x_hi'=2] {'y','x_lo..., dimensions={0} | all-to-all | bytes 524288 | tf_op jit(solution)/shard_map/all_to_all | solution.py:261
  86.6 0.9 shard_map.27
  (1 shorter events, 0.0 us)
Async XLA Ops:
  2.3 19.4 %collective-permute-start.3 = (f32[2,64,2048]{2,1,0:T(8,128)S(1)}, f32[2,64,2048]{2,1,0:T(8,128)S(1)}, u32[]{:S(2)}, u32[]{:S(2)}) collective-permute-start(f32[2,64,2048]{2,1,0:T(8,128)S(1)} %shard_map.18), channel_id=1, source_target_pairs={{2,4},{4,2},{3,5},{5,3},{10,12},{12,10},{11,13},{13,11},{18,20},{2... | collective-permute-start | bytes 3145736 | tf_op jit(solution)/shard_map/ppermute | solution.py:245
  3.0 31.0 %collective-permute-start = (f32[2,64,1024]{2,1,0:T(8,128)S(1)}, f32[2,64,1024]{2,1,0:T(8,128)S(1)}, u32[]{:S(2)}, u32[]{:S(2)}) collective-permute-start(f32[2,64,1024]{2,1,0:T(8,128)S(1)} %shard_map.17), channel_id=1, source_target_pairs={{0,3},{1,2},{2,1},{3,0},{4,7},{5,6},{6,5},{7,4},{8,11},{9,10},{10,... | collective-permute-start | bytes 1572872 | tf_op jit(solution)/shard_map/ppermute | solution.py:236
  14.1 20.1 %collective-permute-start.1 = (f32[2,64,1024]{2,1,0:T(8,128)S(1)}, f32[2,64,1024]{2,1,0:T(8,128)S(1)}, u32[]{:S(2)}, u32[]{:S(2)}) collective-permute-start(f32[2,64,1024]{2,1,0:T(8,128)S(1)} %get-tuple-element.25), channel_id=1, source_target_pairs={{0,2},{1,3},{2,0},{3,1},{4,6},{5,7},{6,4},{7,5},{8,10},{9,11},{10,... | collective-permute-start | bytes 1572872 | tf_op jit(solution)/shard_map/ppermute | solution.py:236
  16.0 19.7 %collective-permute-start.2 = (f32[2,64,1024]{2,1,0:T(8,128)S(1)}, f32[2,64,1024]{2,1,0:T(8,128)S(1)}, u32[]{:S(2)}, u32[]{:S(2)}) collective-permute-start(f32[2,64,1024]{2,1,0:T(8,128)S(1)} %get-tuple-element.26), channel_id=1, source_target_pairs={{0,1},{1,0},{2,3},{3,2},{4,5},{5,4},{6,7},{7,6},{8,9},{9,8},{10,11... | collective-permute-start | bytes 1572872 | tf_op jit(solution)/shard_map/ppermute | solution.py:236
  21.8 43.2 %collective-permute-start.4 = (f32[2,64,2048]{2,1,0:T(8,128)S(1)}, f32[2,64,2048]{2,1,0:T(8,128)S(1)}, u32[]{:S(2)}, u32[]{:S(2)}) collective-permute-start(f32[2,64,2048]{2,1,0:T(8,128)S(1)} %shard_map.24), channel_id=1, source_target_pairs={{0,4},{6,2},{4,6},{2,0},{1,5},{7,3},{5,7},{3,1},{8,12},{14,10},{12... | collective-permute-start | bytes 3145736 | tf_op jit(solution)/shard_map/ppermute | solution.py:254

commit v3 on v2

--- a/solution.py
+++ b/solution.py
@@ -17,9 +17,10 @@
 HBM = pl.BlockSpec(memory_space=pltpu.HBM)
 
 
-def call(kernel, shapes, *args):
+def call(kernel, shapes, *args, cost=None):
     return pl.pallas_call(
         kernel,
+        cost_estimate=cost,
         out_shape=shapes,
         in_specs=[VMEM] * len(args),
         out_specs=jax.tree.map(lambda _: VMEM, shapes),
@@ -40,6 +41,10 @@
 
 def dot(left, right):
     return lax.dot_general(left, right, (((1,), (1,)), ((), ())), preferred_element_type=jnp.float32)
+
+
+def four_passes(passes):
+    return passes[:128, :128] + (passes[:128, 128:] + passes[128:, :128]) + passes[128:, 128:]
 
 
 def complex_tile(products):
@@ -129,102 +134,111 @@
     )(second, passing)
 
 
-def row_of(column):
+PAIRS = ((1, 0), (1, 2), (2, 0), (2, 1), (3, 0), (3, 1))
+
+
+def pair_place(offset, k):
+    high = 1 if k == 1 else 2
+    return PAIRS.index((k, offset if offset & high == 0 else offset ^ k))
+
+
+def is_second(k):
+    return (member_index() & (1 if k == 1 else 2)) != 0
+
+
+def own_kernel(templates_ref, own_ref, shares_ref):
+    at = pl.multiple_of(jnp.where(is_middle(), 2048, 0), 2048)
+    own_ref[...] = jnp.concatenate(split(templates_ref[:, :, pl.ds(at, 2048)].reshape(128, 2048)), axis=0)
+    rows = jnp.concatenate(split(templates_ref[...].reshape(128, 4096)), axis=0)
+    tile = complex_tile(four_passes(dot(rows, rows)))
     row = lax.broadcasted_iota(jnp.int32, (64, 128), 0)
     lane = lax.broadcasted_iota(jnp.int32, (64, 128), 1)
-    return jnp.sum(jnp.where(row == lane, column, 0.0), axis=0, keepdims=True)
-
-
-def own_kernel(templates_ref, own_ref, energy_ref):
-    at = pl.multiple_of(jnp.where(is_middle(), 2048, 0), 2048)
-    high, low = split(templates_ref[:, :, pl.ds(at, 2048)].reshape(128, 2048))
-    own_ref[:128, :] = high
-    own_ref[128:, :] = low
-    squares = jnp.zeros((64, 128), jnp.float32)
-    for start in range(0, 4096, 128):
-        for part in range(2):
-            values = templates_ref[part, :, start : start + 128] * SCALE
-            squares = squares + values * values
-    energy_ref[...] = jnp.zeros((8, 128), jnp.float32)
-    energy_ref[:1, :] = row_of(jnp.sum(squares, axis=1, keepdims=True))
-
-
-def near_kernel(own_ref, three_ref, two_ref, one_ref, out_ref):
+    energies = jnp.sum(jnp.where(row == lane, tile, 0.0), axis=0, keepdims=True)
+    for place in range(16):
+        shares_ref[place, :4, :] = tile[4 * place : 4 * place + 4]
+        shares_ref[place, 4:5, :] = energies
+        shares_ref[place, 5:, :] = jnp.zeros((3, 128), jnp.float32)
+
+
+def near_kernel(itself_ref, own_ref, three_ref, two_ref, one_ref, out_ref):
     blocks = [own_ref[...], one_ref[...], two_ref[...], three_ref[...]]
     rows = jnp.concatenate([block.reshape(128, 1024) for block in blocks], axis=0)
     high, low = split(rows)
     products = dot(high, high) + dot(high, low) + dot(low, high)
-    row = lax.broadcasted_iota(jnp.int32, (64, 128), 0)
-    lane = lax.broadcasted_iota(jnp.int32, (64, 128), 1)
-    energies = []
-    for a in range(4):
-        for k in range(4):
-            b = a ^ k
-            tile = complex_tile(products[128 * a : 128 * a + 128, 128 * b : 128 * b + 128])
-            if k == 0:
-                energies.append(jnp.sum(jnp.where(row == lane, tile, 0.0), axis=0, keepdims=True))
-            at = 16 * a + 8 * (k % 2)
-            for group in range(8):
-                out_ref[2 * group + k // 2, at : at + 8, :] = tile[8 * group : 8 * group + 8]
-    energies = jnp.concatenate(energies + [jnp.zeros((4, 128), jnp.float32)], axis=0)
-    for place in range(16):
-        out_ref[place, 64:, :] = energies
-
-
-def sum_kernel(spread_ref, out_ref):
-    total = spread_ref[0]
-    for place in range(1, 16):
-        total = total + spread_ref[place]
+
+    def tile_of(a, b):
+        return complex_tile(products[128 * a : 128 * a + 128, 128 * b : 128 * b + 128])
+
+    for place, (k, offset) in enumerate(PAIRS):
+        tile = jnp.where(is_second(k), tile_of(offset ^ k, offset), tile_of(offset, offset ^ k))
+        for to in range(16):
+            out_ref[to, 4 * place : 4 * place + 4, :] = tile[4 * to : 4 * to + 4]
+    out_ref[:, 24:, :] = itself_ref[...]
+
+
+def total_of(ref):
+    total = ref[0]
+    for place in range(1, ref.shape[0]):
+        total = total + ref[place]
+    return total
+
+
+def sum_kernel(spread_ref, out_ref, itself_ref):
+    total = total_of(spread_ref)
+    itself_ref[...] = total[24:]
+    energies = total[28:29]
     for offset in range(4):
         to = member_index() ^ offset
-        out_ref[to, :16, :] = total[16 * offset : 16 * offset + 16]
-        for k in range(4):
-            out_ref[to, 16 + k : 17 + k, :] = total[64 + (offset ^ k) : 65 + (offset ^ k)]
-        out_ref[to, 20:, :] = jnp.zeros((4, 128), jnp.float32)
-
-
-def far_kernel(own_ref, energy_ref, far_ref, out_ref):
+        for k in range(1, 4):
+            at = 4 * pair_place(offset, k)
+            out_ref[to, 4 * k - 4 : 4 * k, :] = total[at : at + 4]
+        out_ref[to, 12:13, :] = energies
+        out_ref[to, 13:, :] = jnp.zeros((3, 128), jnp.float32)
+
+
+def far_kernel(near_ref, own_ref, far_ref, out_ref):
     side = lax.axis_index("z1")
-    passes = dot(own_ref[...], jnp.concatenate(split(far_ref[...].reshape(128, 2048)), axis=0))
-    products = passes[:128, :128] + (passes[:128, 128:] + passes[128:, :128]) + passes[128:, 128:]
+    far = jnp.concatenate(split(far_ref[...].reshape(128, 2048)), axis=0)
+    products = four_passes(dot(own_ref[...], far))
     here = complex_tile(products)
     there = complex_tile(products.T)
+    energies = near_ref[member_index(), 12:13, :]
     for quarter in range(4):
         same = 4 * side + quarter
         other = 4 * (1 - side) + quarter
         out_ref[same, :16, :] = here[16 * quarter : 16 * quarter + 16]
         out_ref[other, :16, :] = there[16 * quarter : 16 * quarter + 16]
         out_ref[same, 16:, :] = jnp.zeros((8, 128), jnp.float32)
-        out_ref[other, 16:, :] = energy_ref[...]
-
-
-def pack_kernel(near_ref, far_ref, out_ref):
-    far = far_ref[0]
-    for place in range(1, 8):
-        far = far + far_ref[place]
-    near = near_ref[0, :16, :] + near_ref[1, :16, :] + near_ref[2, :16, :] + near_ref[3, :16, :]
-    near = jnp.concatenate([modulus(near[:8]), modulus(near[8:])], axis=1)
+        out_ref[other, 16:17, :] = energies
+        out_ref[other, 17:, :] = jnp.zeros((7, 128), jnp.float32)
+
+
+def pack_kernel(near_ref, itself_ref, far_ref, out_ref):
+    far = total_of(far_ref)[:16]
+    near = total_of(near_ref)
+    tiles = [itself_ref[:4, :]] + [near[4 * k - 4 : 4 * k] for k in range(1, 4)]
+    tiles = [modulus(tile) for tile in tiles]
+    first = jnp.concatenate(tiles[:2], axis=1)
+    second = jnp.concatenate(tiles[2:], axis=1)
     for place in range(16):
-        out_ref[place, :16, :] = far[:16]
-        out_ref[place, 16:24, :] = near
-        out_ref[place, 24:, :] = far[16:]
-
-
-def final_kernel(near_ref, shares_ref, out_ref):
-    energies = near_ref[0, 16:, :64] + near_ref[1, 16:, :64] + near_ref[2, 16:, :64] + near_ref[3, 16:, :64]
-    far_energies = shares_ref[0, 24:, :64]
-    for place in range(1, 16):
-        far_energies = far_energies + shares_ref[place, 24:, :64]
-    inverse = 1.0 / jnp.sqrt(energies + EPSILON)
-    far_inverse = 1.0 / jnp.sqrt(far_energies * 0.25 + EPSILON)
-    columns = [inverse[k : k + 1] for k in range(4)] + [far_inverse[:1]]
+        out_ref[place, :16, :] = far
+        out_ref[place, 16:20, :] = first
+        out_ref[place, 20:, :] = second
+
+
+def final_kernel(near_ref, far_ref, shares_ref, out_ref):
+    energies = [near_ref[member_index() ^ k, 12:13, :64] for k in range(4)]
+    energies.append(total_of(far_ref)[16:17, :64] * 0.25)
+    columns = [1.0 / jnp.sqrt(energy + EPSILON) for energy in energies]
     diagonal = lax.broadcasted_iota(jnp.int32, (64, 64), 0) == lax.broadcasted_iota(jnp.int32, (64, 64), 1)
     rows = jnp.sum(jnp.where(diagonal, columns[0], 0.0), axis=1, keepdims=True)
     for k in range(5):
         if k < 4:
-            at = 64 * (k % 2)
-            tile = [shares_ref[2 * group + k // 2, 16:24, at : at + 64] for group in range(8)]
+            at, lane = 16 + 4 * (k // 2), 64 * (k % 2)
+            tile = [shares_ref[place, at : at + 4, lane : lane + 64] for place in range(16)]
             tile = jnp.concatenate(tile, axis=0)
+            if k > 0:
+                tile = jnp.where(is_second(k), tile.T, tile)
         else:
             far = [sum(shares_ref[4 * y + quarter, :16, :] for y in range(4)) for quarter in range(4)]
             tile = modulus(jnp.concatenate(far, axis=0))
@@ -248,18 +262,21 @@
     two = swapped(quarter, 2)
     one = swapped(other, 1)
     blocks = [mine, three, two, one]
-    own, energy = call(own_kernel, (jax.ShapeDtypeStruct((256, 2048), jnp.bfloat16), f32(8, 128)), templates)
     second = half(templates, 2048)
+    second, templates = lax.optimization_barrier((second, templates))
+    own, shares = call(own_kernel, (jax.ShapeDtypeStruct((256, 2048), jnp.bfloat16), f32(16, 8, 128)), templates)
     second, passing, own = lax.optimization_barrier((second, passing, own))
     onward = lax.ppermute(choose(second, passing), ("z1", "z0"), [(0, 2), (3, 1), (2, 3), (1, 0)])
 
     blocks, own = lax.optimization_barrier((blocks, own))
-    spread = lax.all_to_all(call(near_kernel, f32(16, 72, 128), *blocks), BAND, 0, 0)
-    near = lax.all_to_all(call(sum_kernel, f32(4, 24, 128), spread), QUAD, 0, 0)
+    cost = pl.CostEstimate(flops=46 * 10**9, bytes_accessed=4 * 2**20, transcendentals=0)
+    spread = lax.all_to_all(call(near_kernel, f32(16, 32, 128), shares, *blocks, cost=cost), BAND, 0, 0)
+    to_quad, itself = call(sum_kernel, (f32(4, 16, 128), f32(8, 128)), spread)
+    near = lax.all_to_all(to_quad, QUAD, 0, 0)
     near, own = lax.optimization_barrier((near, own))
-    far = lax.all_to_all(call(far_kernel, f32(8, 24, 128), own, energy, onward), FAR, 0, 0)
-    shares = lax.all_to_all(call(pack_kernel, f32(16, 32, 128), near, far), BAND, 0, 0)
-    return call(final_kernel, f32(5, 64, 64), near, shares).transpose(1, 0, 2)
+    far = lax.all_to_all(call(far_kernel, f32(8, 24, 128), near, own, onward), FAR, 0, 0)
+    shares = lax.all_to_all(call(pack_kernel, f32(16, 24, 128), near, itself, far), BAND, 0, 0)
+    return call(final_kernel, f32(5, 64, 64), near, far, shares).transpose(1, 0, 2)
 
 
 def solution(mesh):

time: 88 us -> 83.9 us (0.953)
  blocking collectives: 48.1 us -> 44.1 us
    all_to_all x4, blocking collectives: 48.1 us -> 44.1 us  [the longest x1 12.9 us: local(): lax.all_to_all(call(near_kernel, f32(16, 32, 128), shares, *blocks, cost=...]
  transfers between devices with their start and end apart: 5 -> 5, of which waited for: 2 -> 2; matrix products, arithmetic and copies ran while one was open for 0% -> 0% of each run, Pallas kernels for 8% -> 9%
where the time goes in v3:
time: 83.9 us; the launch traced here: 83.4 us
  blocking collectives  44.1 us (53%)
  starting transfers between devices  26.2 us (31%)
  Pallas kernels  11.4 us (14%)
  waiting for transfers between devices  1.67 us (2%)
    ppermute x3, starting transfers between devices, swapped(): return lax.ppermute(value, QUAD, pairs)  13.8 us
    all_to_all x1, blocking collectives, local(): lax.all_to_all(call(near_kernel, f32(16, 32, 128), shares, *blocks, cost=...  12.9 us
    ppermute x1, starting transfers between devices, local(): lax.ppermute(choose(second, passing), ('z1', 'z0'), [(0, 2), (3, 1), (2,...  11.7 us
    all_to_all x1, blocking collectives, local(): lax.all_to_all(call(far_kernel, f32(8, 24, 128), near, own, onward), FAR,...  10.9 us
    all_to_all x1, blocking collectives, local(): near = lax.all_to_all(to_quad, QUAD, 0, 0)  10.3 us
    all_to_all x1, blocking collectives, local(): lax.all_to_all(call(pack_kernel, f32(16, 24, 128), near, itself, far), BA...  9.94 us
    pallas_call x6, Pallas kernels, call(): pl.pallas_call(kernel, cost_estimate=cost, out_shape=shapes, in_specs=[VM...  6.39 us
    pallas_call x2, Pallas kernels, half(): pl.pallas_call(functools.partial(half_kernel, at), out_shape=f32(2, 64, 2...  2.47 us
  transfers between devices with their start and end apart: 5, of which 2 were waited for; matrix products, arithmetic and copies ran while one was open for 0% of the time, Pallas kernels for 9%

profile of v3, /device:TPU:1, one launch (start us, length us, event | category | flops | bytes accessed | tf_op | source)
XLA Modules:
  0.0 83.4 jit_solution(2783872316835147893)
XLA Ops:
  0.0 1.0 %shard_map.17 = f32[2,64,1024]{2,1,0:T(8,128)S(1)} custom-call(f32[2,64,4096]{2,1,0:T(8,128)} %templates_ref.5), custom_call_target="tpu_custom_call" | custom-call | tf_op jit(solution)/shard_map/pallas_call | solution.py:102
  1.1 1.2 %shard_map.18 = f32[2,64,2048]{2,1,0:T(8,128)S(1)} custom-call(f32[2,64,4096]{2,1,0:T(8,128)} %templates_ref.5), custom_call_target="tpu_custom_call" | custom-call | tf_op jit(solution)/shard_map/pallas_call | solution.py:80
  2.3 0.7 collective-permute-start.3
  3.0 9.7 %collective-permute-start = (f32[2,64,1024]{2,1,0:T(8,128)S(1)}, f32[2,64,1024]{2,1,0:T(8,128)S(1)}, u32[]{:S(2)}, u32[]{:S(2)}) collective-permute-start(f32[2,64,1024]{2,1,0:T(8,128)S(1)} %shard_map.17), channel_id=1, source_target_pairs={{0,3},{1,2},{2,1},{3,0},{4,7},{5,6},{6,5},{7,4},{8,11},{9,10},{10,... | collective-permute-start | bytes 1572872 | tf_op jit(solution)/shard_map/ppermute | solution.py:250
  12.7 1.4 %shard_map.21 = (f32[2,64,1024]{2,1,0:T(8,128)S(1)}, f32[2,64,1024]{2,1,0:T(8,128)S(1)}, f32[2,64,1024]{2,1,0:T(8,128)S(1)}) custom-call(f32[2,64,4096]{2,1,0:T(8,128)} %templates_ref.5), custom_call_target="tpu_custom_call" | custom-call | tf_op jit(solution)/shard_map/pallas_call | solution.py:102
  14.1 1.9 %collective-permute-start.1 = (f32[2,64,1024]{2,1,0:T(8,128)S(1)}, f32[2,64,1024]{2,1,0:T(8,128)S(1)}, u32[]{:S(2)}, u32[]{:S(2)}) collective-permute-start(f32[2,64,1024]{2,1,0:T(8,128)S(1)} %get-tuple-element.31), channel_id=1, source_target_pairs={{0,2},{1,3},{2,0},{3,1},{4,6},{5,7},{6,4},{7,5},{8,10},{9,11},{10,... | collective-permute-start | bytes 1572872 | tf_op jit(solution)/shard_map/ppermute | solution.py:250
  16.0 2.2 %collective-permute-start.2 = (f32[2,64,1024]{2,1,0:T(8,128)S(1)}, f32[2,64,1024]{2,1,0:T(8,128)S(1)}, u32[]{:S(2)}, u32[]{:S(2)}) collective-permute-start(f32[2,64,1024]{2,1,0:T(8,128)S(1)} %get-tuple-element.32), channel_id=1, source_target_pairs={{0,1},{1,0},{2,3},{3,2},{4,5},{5,4},{6,7},{7,6},{8,9},{9,8},{10,11... | collective-permute-start | bytes 1572872 | tf_op jit(solution)/shard_map/ppermute | solution.py:250
  18.2 1.2 %shard_map.19.second_ref = f32[2,64,2048]{2,1,0:T(8,128)S(1)} custom-call(f32[2,64,4096]{2,1,0:T(8,128)} %templates_ref.5), custom_call_target="tpu_custom_call" | custom-call | tf_op jit(solution)/shard_map/pallas_call | solution.py:80
  19.5 2.8 %shard_map.20 = (bf16[256,2048]{1,0:T(8,128)(2,1)S(1)}, f32[16,8,128]{2,1,0:T(8,128)S(1)}) custom-call(f32[2,64,4096]{2,1,0:T(8,128)} %templates_ref.5), custom_call_target="tpu_custom_call" | custom-call | tf_op jit(solution)/shard_map/pallas_call | solution.py:21
  22.3 0.0 collective-permute-done.3.passing_ref
  22.3 0.1 shard_map.24
  22.4 11.7 %collective-permute-start.4 = (f32[2,64,2048]{2,1,0:T(8,128)S(1)}, f32[2,64,2048]{2,1,0:T(8,128)S(1)}, u32[]{:S(2)}, u32[]{:S(2)}) collective-permute-start(f32[2,64,2048]{2,1,0:T(8,128)S(1)} %shard_map.24), channel_id=1, source_target_pairs={{0,4},{6,2},{4,6},{2,0},{1,5},{7,3},{5,7},{3,1},{8,12},{14,10},{12... | collective-permute-start | bytes 3145736 | tf_op jit(solution)/shard_map/ppermute | solution.py:269
  34.0 0.0 collective-permute-done.three_ref
  34.1 0.2 collective-permute-done.1.two_ref
  34.2 1.5 %collective-permute-done.2.one_ref = f32[2,64,1024]{2,1,0:T(8,128)S(1)} collective-permute-done((f32[2,64,1024]{2,1,0:T(8,128)S(1)}, f32[2,64,1024]{2,1,0:T(8,128)S(1)}, u32[]{:S(2)}, u32[]{:S(2)}) %collective-permute-start.2) | collective-permute-done | bytes 524320 | tf_op jit(solution)/shard_map/ppermute | solution.py:250
  35.7 1.9 %shard_map.22 = f32[16,32,128]{2,1,0:T(8,128)S(1)} custom-call(f32[16,8,128]{2,1,0:T(8,128)S(1)} %get-tuple-element.29.itself_ref, f32[2,64,1024]{2,1,0:T(8,128)S(1)} %get-tuple-element.36.own_ref, f32[2,64,1024]{2,1,0:T(8,128)S(1)} %collective-permute-done.three_ref, f32[2,64,1024]{2,1,0:T(8,128)S(1)} %collective-permute-done.1.two_ref, ...), custom_call_target="tpu_custom_call" | custom-call | flops 46000001024 | bytes 4194304 | tf_op jit(solution)/shard_map/pallas_call | solution.py:21
  37.7 12.9 %all_to_all.20.spread_ref = f32[16,32,128]{2,1,0:T(8,128)S(1)} all-to-all(f32[16,32,128]{2,1,0:T(8,128)S(1)} %shard_map.22), channel_id=1, replica_groups=mesh['y'=4,'x_lo'=2,'core'=2,'z_hi'=4,'z1'=2,'z0'=2,'x_hi'=2] {'y','x_lo..., dimensions={0} | all-to-all | bytes 524288 | tf_op jit(solution)/shard_map/all_to_all | solution.py:273
  50.6 10.3 %all_to_all.21.near_ref = f32[4,16,128]{2,1,0:T(8,128)S(1)} all-to-all(f32[4,16,128]{2,1,0:T(8,128)S(1)} %get-tuple-element.40), channel_id=1, replica_groups=mesh['y'=4,'x_lo'=2,'core'=2,'z_hi'=4,'z1'=2,'z0'=2,'x_hi'=2] {'z0','x_hi'}, dimensions={0} | all-to-all | bytes 65536 | tf_op jit(solution)/shard_map/all_to_all | solution.py:275
  60.9 0.0 collective-permute-done.4.far_ref
  60.9 0.6 shard_map.25
  61.5 10.9 %all_to_all.22.far_ref = f32[8,24,128]{2,1,0:T(8,128)S(1)} all-to-all(f32[8,24,128]{2,1,0:T(8,128)S(1)} %shard_map.25), channel_id=1, replica_groups=mesh['y'=4,'x_lo'=2,'core'=2,'z_hi'=4,'z1'=2,'z0'=2,'x_hi'=2] {'z1','x_l..., dimensions={0} | all-to-all | bytes 196608 | tf_op jit(solution)/shard_map/all_to_all | solution.py:277
  72.4 0.2 shard_map.26
  72.6 9.9 %all_to_all.23.shares_ref = f32[16,24,128]{2,1,0:T(8,128)S(1)} all-to-all(f32[16,24,128]{2,1,0:T(8,128)S(1)} %shard_map.26), channel_id=1, replica_groups=mesh['y'=4,'x_lo'=2,'core'=2,'z_hi'=4,'z1'=2,'z0'=2,'x_hi'=2] {'y','x_lo..., dimensions={0} | all-to-all | bytes 393216 | tf_op jit(solution)/shard_map/all_to_all | solution.py:278
  82.5 0.9 %shard_map.27 = f32[5,64,64]{2,1,0:T(8,128)} custom-call(f32[4,16,128]{2,1,0:T(8,128)S(1)} %all_to_all.21.near_ref, f32[8,24,128]{2,1,0:T(8,128)S(1)} %all_to_all.22.far_ref, f32[16,24,128]{2,1,0:T(8,128)S(1)} %all_to_all.23.shares_ref), custom_call_target="tpu_custom_call" | custom-call | tf_op jit(solution)/shard_map/pallas_call | solution.py:21
  (1 shorter events, 0.0 us)
Async XLA Ops:
  2.3 20.0 %collective-permute-start.3 = (f32[2,64,2048]{2,1,0:T(8,128)S(1)}, f32[2,64,2048]{2,1,0:T(8,128)S(1)}, u32[]{:S(2)}, u32[]{:S(2)}) collective-permute-start(f32[2,64,2048]{2,1,0:T(8,128)S(1)} %shard_map.18), channel_id=1, source_target_pairs={{2,4},{4,2},{3,5},{5,3},{10,12},{12,10},{11,13},{13,11},{18,20},{2... | collective-permute-start | bytes 3145736 | tf_op jit(solution)/shard_map/ppermute | solution.py:259
  3.0 31.0 %collective-permute-start = (f32[2,64,1024]{2,1,0:T(8,128)S(1)}, f32[2,64,1024]{2,1,0:T(8,128)S(1)}, u32[]{:S(2)}, u32[]{:S(2)}) collective-permute-start(f32[2,64,1024]{2,1,0:T(8,128)S(1)} %shard_map.17), channel_id=1, source_target_pairs={{0,3},{1,2},{2,1},{3,0},{4,7},{5,6},{6,5},{7,4},{8,11},{9,10},{10,... | collective-permute-start | bytes 1572872 | tf_op jit(solution)/shard_map/ppermute | solution.py:250
  14.1 20.1 %collective-permute-start.1 = (f32[2,64,1024]{2,1,0:T(8,128)S(1)}, f32[2,64,1024]{2,1,0:T(8,128)S(1)}, u32[]{:S(2)}, u32[]{:S(2)}) collective-permute-start(f32[2,64,1024]{2,1,0:T(8,128)S(1)} %get-tuple-element.31), channel_id=1, source_target_pairs={{0,2},{1,3},{2,0},{3,1},{4,6},{5,7},{6,4},{7,5},{8,10},{9,11},{10,... | collective-permute-start | bytes 1572872 | tf_op jit(solution)/shard_map/ppermute | solution.py:250
  16.0 19.7 %collective-permute-start.2 = (f32[2,64,1024]{2,1,0:T(8,128)S(1)}, f32[2,64,1024]{2,1,0:T(8,128)S(1)}, u32[]{:S(2)}, u32[]{:S(2)}) collective-permute-start(f32[2,64,1024]{2,1,0:T(8,128)S(1)} %get-tuple-element.32), channel_id=1, source_target_pairs={{0,1},{1,0},{2,3},{3,2},{4,5},{5,4},{6,7},{7,6},{8,9},{9,8},{10,11... | collective-permute-start | bytes 1572872 | tf_op jit(solution)/shard_map/ppermute | solution.py:250
  22.4 38.5 %collective-permute-start.4 = (f32[2,64,2048]{2,1,0:T(8,128)S(1)}, f32[2,64,2048]{2,1,0:T(8,128)S(1)}, u32[]{:S(2)}, u32[]{:S(2)}) collective-permute-start(f32[2,64,2048]{2,1,0:T(8,128)S(1)} %shard_map.24), channel_id=1, source_target_pairs={{0,4},{6,2},{4,6},{2,0},{1,5},{7,3},{5,7},{3,1},{8,12},{14,10},{12... | collective-permute-start | bytes 3145736 | tf_op jit(solution)/shard_map/ppermute | solution.py:269

commit v4 on v3

--- a/solution.py
+++ b/solution.py
@@ -17,9 +17,10 @@
 HBM = pl.BlockSpec(memory_space=pltpu.HBM)
 
 
-def call(kernel, shapes, *args, cost=None):
+def call(kernel, shapes, *args, cost=None, scratch=()):
     return pl.pallas_call(
         kernel,
+        scratch_shapes=scratch,
         cost_estimate=cost,
         out_shape=shapes,
         in_specs=[VMEM] * len(args),
@@ -70,41 +71,28 @@
     return lax.axis_index("z1") != lax.axis_index("z0")
 
 
-def half_kernel(at, templates_ref, out_ref, sem):
-    copy = pltpu.make_async_copy(templates_ref.at[:, :, at : at + 2048], out_ref, sem)
-    copy.start()
-    copy.wait()
-
-
-def half(templates, at):
-    return pl.pallas_call(
-        functools.partial(half_kernel, at),
-        out_shape=f32(2, 64, 2048),
-        in_specs=[HBM],
-        out_specs=VMEM,
-        scratch_shapes=[pltpu.SemaphoreType.DMA],
-        compiler_params=pltpu.CompilerParams(vmem_limit_bytes=8 * 2**20),
-    )(templates)
-
-
-def quarters_kernel(offsets, templates_ref, *refs):
+def cut_kernel(pieces, templates_ref, *refs):
     copies = []
-    for place, offset in enumerate(offsets):
-        at = pl.multiple_of((member_index() ^ offset) * 1024, 1024)
-        copies.append(pltpu.make_async_copy(templates_ref.at[:, :, pl.ds(at, 1024)], refs[place], refs[-1].at[place]))
+    for place, (kind, which) in enumerate(pieces):
+        if kind == "half":
+            source = templates_ref.at[:, :, 2048 * which : 2048 * which + 2048]
+        else:
+            at = pl.multiple_of((member_index() ^ which) * 1024, 1024)
+            source = templates_ref.at[:, :, pl.ds(at, 1024)]
+        copies.append(pltpu.make_async_copy(source, refs[place], refs[-1].at[place]))
     for copy in copies:
         copy.start()
     for copy in copies:
         copy.wait()
 
 
-def quarters(templates, *offsets):
+def cut(templates, *pieces):
     return pl.pallas_call(
-        functools.partial(quarters_kernel, offsets),
-        out_shape=(f32(2, 64, 1024),) * len(offsets),
+        functools.partial(cut_kernel, pieces),
+        out_shape=tuple(f32(2, 64, 2048 if kind == "half" else 1024) for kind, _ in pieces),
         in_specs=[HBM],
-        out_specs=(VMEM,) * len(offsets),
-        scratch_shapes=[pltpu.SemaphoreType.DMA((len(offsets),))],
+        out_specs=(VMEM,) * len(pieces),
+        scratch_shapes=[pltpu.SemaphoreType.DMA((len(pieces),))],
         compiler_params=pltpu.CompilerParams(vmem_limit_bytes=8 * 2**20),
     )(templates)
 
@@ -134,12 +122,7 @@
     )(second, passing)
 
 
-PAIRS = ((1, 0), (1, 2), (2, 0), (2, 1), (3, 0), (3, 1))
-
-
-def pair_place(offset, k):
-    high = 1 if k == 1 else 2
-    return PAIRS.index((k, offset if offset & high == 0 else offset ^ k))
+PAIRS = ((0, 1), (0, 2), (0, 3), (1, 2), (1, 3), (2, 3))
 
 
 def is_second(k):
@@ -160,19 +143,23 @@
         shares_ref[place, 5:, :] = jnp.zeros((3, 128), jnp.float32)
 
 
-def near_kernel(itself_ref, own_ref, three_ref, two_ref, one_ref, out_ref):
-    blocks = [own_ref[...], one_ref[...], two_ref[...], three_ref[...]]
-    rows = jnp.concatenate([block.reshape(128, 1024) for block in blocks], axis=0)
-    high, low = split(rows)
-    products = dot(high, high) + dot(high, low) + dot(low, high)
-
-    def tile_of(a, b):
-        return complex_tile(products[128 * a : 128 * a + 128, 128 * b : 128 * b + 128])
-
-    for place, (k, offset) in enumerate(PAIRS):
-        tile = jnp.where(is_second(k), tile_of(offset ^ k, offset), tile_of(offset, offset ^ k))
-        for to in range(16):
-            out_ref[to, 4 * place : 4 * place + 4, :] = tile[4 * to : 4 * to + 4]
+def near_kernel(itself_ref, own_ref, three_ref, one_ref, two_ref, out_ref, high_ref, low_ref):
+    for offset, ref in enumerate((own_ref, one_ref, two_ref, three_ref)):
+        high, low = split(ref[...].reshape(128, 1024))
+        high_ref[member_index() ^ offset] = high
+        low_ref[member_index() ^ offset] = low
+    for a in range(3):
+        right_high = high_ref[a + 1 :].reshape(128 * (3 - a), 1024)
+        right_low = low_ref[a + 1 :].reshape(128 * (3 - a), 1024)
+        left = jnp.concatenate([high_ref[a], low_ref[a]], axis=0)
+        passes = dot(left, right_high)
+        products = passes[:128] + passes[128:] + dot(high_ref[a], right_low)
+        for b in range(a + 1, 4):
+            at = 128 * (b - a - 1)
+            tile = complex_tile(products[:, at : at + 128])
+            place = 4 * PAIRS.index((a, b))
+            for to in range(16):
+                out_ref[to, place : place + 4, :] = tile[4 * to : 4 * to + 4]
     out_ref[:, 24:, :] = itself_ref[...]
 
 
@@ -187,10 +174,9 @@
     total = total_of(spread_ref)
     itself_ref[...] = total[24:]
     energies = total[28:29]
-    for offset in range(4):
-        to = member_index() ^ offset
+    for to in range(4):
         for k in range(1, 4):
-            at = 4 * pair_place(offset, k)
+            at = 4 * PAIRS.index((min(to, to ^ k), max(to, to ^ k)))
             out_ref[to, 4 * k - 4 : 4 * k, :] = total[at : at + 4]
         out_ref[to, 12:13, :] = energies
         out_ref[to, 13:, :] = jnp.zeros((3, 128), jnp.float32)
@@ -252,25 +238,25 @@
 
 def local(templates):
     templates = pltpu.with_memory_space_constraint(templates, pltpu.HBM)
-    (quarter,) = quarters(templates, 3)
-    three = swapped(quarter, 3)
-    quarter, templates = lax.optimization_barrier((quarter, templates))
-    first = half(templates, 0)
+    first, third = cut(templates, ("half", 0), ("quarter", 3))
     passing = lax.ppermute(first, ("z1", "z0"), [(1, 2), (2, 1)])
-    first, templates = lax.optimization_barrier((first, templates))
-    mine, other, quarter = quarters(templates, 0, 1, 2)
-    two = swapped(quarter, 2)
-    one = swapped(other, 1)
-    blocks = [mine, three, two, one]
-    second = half(templates, 2048)
+    three = swapped(third, 3)
+    third, templates = lax.optimization_barrier((third, templates))
+    other, nearest, mine = cut(templates, ("quarter", 2), ("quarter", 1), ("quarter", 0))
+    blocks = [mine, three, swapped(nearest, 1), swapped(other, 2)]
+    other, templates = lax.optimization_barrier((other, templates))
+    (second,) = cut(templates, ("half", 1))
     second, templates = lax.optimization_barrier((second, templates))
     own, shares = call(own_kernel, (jax.ShapeDtypeStruct((256, 2048), jnp.bfloat16), f32(16, 8, 128)), templates)
     second, passing, own = lax.optimization_barrier((second, passing, own))
-    onward = lax.ppermute(choose(second, passing), ("z1", "z0"), [(0, 2), (3, 1), (2, 3), (1, 0)])
-
-    blocks, own = lax.optimization_barrier((blocks, own))
+    outgoing = choose(second, passing)
+    onward = lax.ppermute(outgoing, ("z1", "z0"), [(0, 2), (3, 1), (2, 3), (1, 0)])
+
+    blocks, own, outgoing = lax.optimization_barrier((blocks, own, outgoing))
     cost = pl.CostEstimate(flops=46 * 10**9, bytes_accessed=4 * 2**20, transcendentals=0)
-    spread = lax.all_to_all(call(near_kernel, f32(16, 32, 128), shares, *blocks, cost=cost), BAND, 0, 0)
+    terms = (pltpu.VMEM((4, 128, 1024), jnp.bfloat16),) * 2
+    spread = call(near_kernel, f32(16, 32, 128), shares, *blocks, cost=cost, scratch=terms)
+    spread = lax.all_to_all(spread, BAND, 0, 0)
     to_quad, itself = call(sum_kernel, (f32(4, 16, 128), f32(8, 128)), spread)
     near = lax.all_to_all(to_quad, QUAD, 0, 0)
     near, own = lax.optimization_barrier((near, own))

time: 83.9 us -> 82.9 us (0.988)
  Pallas kernels: 11.4 us -> 10.5 us
    pallas_call x10 -> x9, Pallas kernels: 11.3 us -> 10.4 us  [the longest x6 6.36 us: call(): pl.pallas_call(kernel, scratch_shapes=scratch, cost_estimate=cost, out_sh...]
  transfers between devices with their start and end apart: 5 -> 5, of which waited for: 2 -> 1; matrix products, arithmetic and copies ran while one was open for 0% -> 0% of each run, Pallas kernels for 9% -> 9%
where the time goes in v4:
time: 82.9 us; the launch traced here: 82.5 us
  blocking collectives  43.5 us (52%)
  starting transfers between devices  26.1 us (31%)
  Pallas kernels  10.5 us (13%)
  waiting for transfers between devices  2.25 us (3%)
    ppermute x3, starting transfers between devices, swapped(): return lax.ppermute(value, QUAD, pairs)  13.8 us
    all_to_all x1, blocking collectives, local(): spread = lax.all_to_all(spread, BAND, 0, 0)  12.3 us
    ppermute x1, starting transfers between devices, local(): lax.ppermute(outgoing, ('z1', 'z0'), [(0, 2), (3, 1), (2, 3), (1, 0)])  11.7 us
    all_to_all x1, blocking collectives, local(): lax.all_to_all(call(far_kernel, f32(8, 24, 128), near, own, onward), FAR,...  10.9 us
    all_to_all x1, blocking collectives, local(): near = lax.all_to_all(to_quad, QUAD, 0, 0)  10.3 us
    all_to_all x1, blocking collectives, local(): lax.all_to_all(call(pack_kernel, f32(16, 24, 128), near, itself, far), BA...  9.95 us
    pallas_call x6, Pallas kernels, call(): pl.pallas_call(kernel, scratch_shapes=scratch, cost_estimate=cost, out_sh...  6.36 us
    pallas_call x3, Pallas kernels, cut(): pl.pallas_call(functools.partial(cut_kernel, pieces), out_shape=tuple((f3...  4.01 us
  transfers between devices with their start and end apart: 5, of which 1 were waited for; matrix products, arithmetic and copies ran while one was open for 0% of the time, Pallas kernels for 9%

profile of v4, /device:TPU:1, one launch (start us, length us, event | category | flops | bytes accessed | tf_op | source)
XLA Modules:
  0.0 82.5 jit_solution(15327070255780571467)
XLA Ops:
  0.0 1.4 %shard_map.17 = (f32[2,64,2048]{2,1,0:T(8,128)S(1)}, f32[2,64,1024]{2,1,0:T(8,128)S(1)}) custom-call(f32[2,64,4096]{2,1,0:T(8,128)} %templates_ref.4), custom_call_target="tpu_custom_call" | custom-call | tf_op jit(solution)/shard_map/pallas_call | solution.py:90
  1.4 0.7 collective-permute-start.3
  2.1 9.7 %collective-permute-start = (f32[2,64,1024]{2,1,0:T(8,128)S(1)}, f32[2,64,1024]{2,1,0:T(8,128)S(1)}, u32[]{:S(2)}, u32[]{:S(2)}) collective-permute-start(f32[2,64,1024]{2,1,0:T(8,128)S(1)} %get-tuple-element.28), channel_id=1, source_target_pairs={{0,3},{1,2},{2,1},{3,0},{4,7},{5,6},{6,5},{7,4},{8,11},{9,10},{10,... | collective-permute-start | bytes 1572872 | tf_op jit(solution)/shard_map/ppermute | solution.py:236
  11.8 1.4 %shard_map.18 = (f32[2,64,1024]{2,1,0:T(8,128)S(1)}, f32[2,64,1024]{2,1,0:T(8,128)S(1)}, f32[2,64,1024]{2,1,0:T(8,128)S(1)}) custom-call(f32[2,64,4096]{2,1,0:T(8,128)} %templates_ref.4), custom_call_target="tpu_custom_call" | custom-call | tf_op jit(solution)/shard_map/pallas_call | solution.py:90
  13.2 2.1 %collective-permute-start.1 = (f32[2,64,1024]{2,1,0:T(8,128)S(1)}, f32[2,64,1024]{2,1,0:T(8,128)S(1)}, u32[]{:S(2)}, u32[]{:S(2)}) collective-permute-start(f32[2,64,1024]{2,1,0:T(8,128)S(1)} %get-tuple-element.35), channel_id=1, source_target_pairs={{0,1},{1,0},{2,3},{3,2},{4,5},{5,4},{6,7},{7,6},{8,9},{9,8},{10,11... | collective-permute-start | bytes 1572872 | tf_op jit(solution)/shard_map/ppermute | solution.py:236
  15.3 2.0 %collective-permute-start.2 = (f32[2,64,1024]{2,1,0:T(8,128)S(1)}, f32[2,64,1024]{2,1,0:T(8,128)S(1)}, u32[]{:S(2)}, u32[]{:S(2)}) collective-permute-start(f32[2,64,1024]{2,1,0:T(8,128)S(1)} %get-tuple-element.30), channel_id=1, source_target_pairs={{0,2},{1,3},{2,0},{3,1},{4,6},{5,7},{6,4},{7,5},{8,10},{9,11},{10,... | collective-permute-start | bytes 1572872 | tf_op jit(solution)/shard_map/ppermute | solution.py:236
  17.3 1.2 %shard_map.19.second_ref = f32[2,64,2048]{2,1,0:T(8,128)S(1)} custom-call(f32[2,64,4096]{2,1,0:T(8,128)} %templates_ref.4), custom_call_target="tpu_custom_call" | custom-call | tf_op jit(solution)/shard_map/pallas_call | solution.py:90
  18.6 2.8 %shard_map.20 = (bf16[256,2048]{1,0:T(8,128)(2,1)S(1)}, f32[16,8,128]{2,1,0:T(8,128)S(1)}) custom-call(f32[2,64,4096]{2,1,0:T(8,128)} %templates_ref.4), custom_call_target="tpu_custom_call" | custom-call | tf_op jit(solution)/shard_map/pallas_call | solution.py:21
  21.3 0.0 collective-permute-done.3.passing_ref
  21.4 0.1 shard_map.21
  21.5 11.7 %collective-permute-start.4 = (f32[2,64,2048]{2,1,0:T(8,128)S(1)}, f32[2,64,2048]{2,1,0:T(8,128)S(1)}, u32[]{:S(2)}, u32[]{:S(2)}) collective-permute-start(f32[2,64,2048]{2,1,0:T(8,128)S(1)} %shard_map.21), channel_id=1, source_target_pairs={{0,4},{6,2},{4,6},{2,0},{1,5},{7,3},{5,7},{3,1},{8,12},{14,10},{12... | collective-permute-start | bytes 3145736 | tf_op jit(solution)/shard_map/ppermute | solution.py:253
  33.1 0.0 collective-permute-done.three_ref
  33.1 2.2 %collective-permute-done.1.one_ref = f32[2,64,1024]{2,1,0:T(8,128)S(1)} collective-permute-done((f32[2,64,1024]{2,1,0:T(8,128)S(1)}, f32[2,64,1024]{2,1,0:T(8,128)S(1)}, u32[]{:S(2)}, u32[]{:S(2)}) %collective-permute-start.1) | collective-permute-done | bytes 524320 | tf_op jit(solution)/shard_map/ppermute | solution.py:236
  35.4 0.0 collective-permute-done.2.two_ref
  35.4 1.9 %shard_map.22 = f32[16,32,128]{2,1,0:T(8,128)S(1)} custom-call(f32[16,8,128]{2,1,0:T(8,128)S(1)} %get-tuple-element.33.itself_ref, f32[2,64,1024]{2,1,0:T(8,128)S(1)} %get-tuple-element.42.own_ref, f32[2,64,1024]{2,1,0:T(8,128)S(1)} %collective-permute-done.three_ref, f32[2,64,1024]{2,1,0:T(8,128)S(1)} %collective-permute-done.1.one_ref, ...), custom_call_target="tpu_custom_call" | custom-call | flops 46000001024 | bytes 4194304 | tf_op jit(solution)/shard_map/pallas_call | solution.py:21
  37.3 12.3 %all_to_all.20.spread_ref = f32[16,32,128]{2,1,0:T(8,128)S(1)} all-to-all(f32[16,32,128]{2,1,0:T(8,128)S(1)} %shard_map.22), channel_id=1, replica_groups=mesh['y'=4,'x_lo'=2,'core'=2,'z_hi'=4,'z1'=2,'z0'=2,'x_hi'=2] {'y','x_lo..., dimensions={0} | all-to-all | bytes 524288 | tf_op jit(solution)/shard_map/all_to_all | solution.py:259
  49.6 10.3 %all_to_all.21.near_ref = f32[4,16,128]{2,1,0:T(8,128)S(1)} all-to-all(f32[4,16,128]{2,1,0:T(8,128)S(1)} %get-tuple-element.46), channel_id=1, replica_groups=mesh['y'=4,'x_lo'=2,'core'=2,'z_hi'=4,'z1'=2,'z0'=2,'x_hi'=2] {'z0','x_hi'}, dimensions={0} | all-to-all | bytes 65536 | tf_op jit(solution)/shard_map/all_to_all | solution.py:261
  59.9 0.0 collective-permute-done.4.far_ref
  59.9 0.6 shard_map.24
  60.6 10.9 %all_to_all.22.far_ref = f32[8,24,128]{2,1,0:T(8,128)S(1)} all-to-all(f32[8,24,128]{2,1,0:T(8,128)S(1)} %shard_map.24), channel_id=1, replica_groups=mesh['y'=4,'x_lo'=2,'core'=2,'z_hi'=4,'z1'=2,'z0'=2,'x_hi'=2] {'z1','x_l..., dimensions={0} | all-to-all | bytes 196608 | tf_op jit(solution)/shard_map/all_to_all | solution.py:263
  71.5 0.2 shard_map.25
  71.7 9.9 %all_to_all.23.shares_ref = f32[16,24,128]{2,1,0:T(8,128)S(1)} all-to-all(f32[16,24,128]{2,1,0:T(8,128)S(1)} %shard_map.25), channel_id=1, replica_groups=mesh['y'=4,'x_lo'=2,'core'=2,'z_hi'=4,'z1'=2,'z0'=2,'x_hi'=2] {'y','x_lo..., dimensions={0} | all-to-all | bytes 393216 | tf_op jit(solution)/shard_map/all_to_all | solution.py:264
  81.6 0.9 %shard_map.26 = f32[5,64,64]{2,1,0:T(8,128)} custom-call(f32[4,16,128]{2,1,0:T(8,128)S(1)} %all_to_all.21.near_ref, f32[8,24,128]{2,1,0:T(8,128)S(1)} %all_to_all.22.far_ref, f32[16,24,128]{2,1,0:T(8,128)S(1)} %all_to_all.23.shares_ref), custom_call_target="tpu_custom_call" | custom-call | tf_op jit(solution)/shard_map/pallas_call | solution.py:21
  (1 shorter events, 0.0 us)
Async XLA Ops:
  1.4 20.0 %collective-permute-start.3 = (f32[2,64,2048]{2,1,0:T(8,128)S(1)}, f32[2,64,2048]{2,1,0:T(8,128)S(1)}, u32[]{:S(2)}, u32[]{:S(2)}) collective-permute-start(f32[2,64,2048]{2,1,0:T(8,128)S(1)} %get-tuple-element.37), channel_id=1, source_target_pairs={{2,4},{4,2},{3,5},{5,3},{10,12},{12,10},{11,13},{13,11},{18,20},{2... | collective-permute-start | bytes 3145736 | tf_op jit(solution)/shard_map/ppermute | solution.py:242
  2.1 31.0 %collective-permute-start = (f32[2,64,1024]{2,1,0:T(8,128)S(1)}, f32[2,64,1024]{2,1,0:T(8,128)S(1)}, u32[]{:S(2)}, u32[]{:S(2)}) collective-permute-start(f32[2,64,1024]{2,1,0:T(8,128)S(1)} %get-tuple-element.28), channel_id=1, source_target_pairs={{0,3},{1,2},{2,1},{3,0},{4,7},{5,6},{6,5},{7,4},{8,11},{9,10},{10,... | collective-permute-start | bytes 1572872 | tf_op jit(solution)/shard_map/ppermute | solution.py:236
  13.2 22.2 %collective-permute-start.1 = (f32[2,64,1024]{2,1,0:T(8,128)S(1)}, f32[2,64,1024]{2,1,0:T(8,128)S(1)}, u32[]{:S(2)}, u32[]{:S(2)}) collective-permute-start(f32[2,64,1024]{2,1,0:T(8,128)S(1)} %get-tuple-element.35), channel_id=1, source_target_pairs={{0,1},{1,0},{2,3},{3,2},{4,5},{5,4},{6,7},{7,6},{8,9},{9,8},{10,11... | collective-permute-start | bytes 1572872 | tf_op jit(solution)/shard_map/ppermute | solution.py:236
  15.3 20.1 %collective-permute-start.2 = (f32[2,64,1024]{2,1,0:T(8,128)S(1)}, f32[2,64,1024]{2,1,0:T(8,128)S(1)}, u32[]{:S(2)}, u32[]{:S(2)}) collective-permute-start(f32[2,64,1024]{2,1,0:T(8,128)S(1)} %get-tuple-element.30), channel_id=1, source_target_pairs={{0,2},{1,3},{2,0},{3,1},{4,6},{5,7},{6,4},{7,5},{8,10},{9,11},{10,... | collective-permute-start | bytes 1572872 | tf_op jit(solution)/shard_map/ppermute | solution.py:236
  21.5 38.5 %collective-permute-start.4 = (f32[2,64,2048]{2,1,0:T(8,128)S(1)}, f32[2,64,2048]{2,1,0:T(8,128)S(1)}, u32[]{:S(2)}, u32[]{:S(2)}) collective-permute-start(f32[2,64,2048]{2,1,0:T(8,128)S(1)} %shard_map.21), channel_id=1, source_target_pairs={{0,4},{6,2},{4,6},{2,0},{1,5},{7,3},{5,7},{3,1},{8,12},{14,10},{12... | collective-permute-start | bytes 3145736 | tf_op jit(solution)/shard_map/ppermute | solution.py:253

commit v5 on v4

--- a/solution.py
+++ b/solution.py
@@ -148,18 +148,21 @@
         high, low = split(ref[...].reshape(128, 1024))
         high_ref[member_index() ^ offset] = high
         low_ref[member_index() ^ offset] = low
-    for a in range(3):
-        right_high = high_ref[a + 1 :].reshape(128 * (3 - a), 1024)
-        right_low = low_ref[a + 1 :].reshape(128 * (3 - a), 1024)
-        left = jnp.concatenate([high_ref[a], low_ref[a]], axis=0)
-        passes = dot(left, right_high)
-        products = passes[:128] + passes[128:] + dot(high_ref[a], right_low)
-        for b in range(a + 1, 4):
-            at = 128 * (b - a - 1)
-            tile = complex_tile(products[:, at : at + 128])
-            place = 4 * PAIRS.index((a, b))
-            for to in range(16):
-                out_ref[to, place : place + 4, :] = tile[4 * to : 4 * to + 4]
+
+    def both(a):
+        return jnp.concatenate([high_ref[a], low_ref[a]], axis=0)
+
+    left = jnp.concatenate([high_ref[0], high_ref[1], low_ref[0], low_ref[1]], axis=0)
+    passes = dot(left, jnp.concatenate([high_ref[2], high_ref[3]], axis=0))
+    across = dot(left[:256], jnp.concatenate([low_ref[2], low_ref[3]], axis=0)) + passes[256:] + passes[:256]
+    products = {(0, 1): four_passes(dot(both(0), both(1))), (2, 3): four_passes(dot(both(2), both(3)))}
+    for a in range(2):
+        for b in range(2):
+            products[a, b + 2] = across[128 * a : 128 * a + 128, 128 * b : 128 * b + 128]
+    for place, pair in enumerate(PAIRS):
+        tile = complex_tile(products[pair])
+        for to in range(16):
+            out_ref[to, 4 * place : 4 * place + 4, :] = tile[4 * to : 4 * to + 4]
     out_ref[:, 24:, :] = itself_ref[...]
 
 

time: 82.9 us -> 82.9 us (level)
  no operation moved by 1% of the time
where the time goes in v5:
time: 82.9 us; the launch traced here: 82.5 us
  blocking collectives  43.8 us (53%)
  starting transfers between devices  26.1 us (31%)
  Pallas kernels  10.2 us (12%)
  waiting for transfers between devices  2.25 us (3%)
    ppermute x3, starting transfers between devices, swapped(): return lax.ppermute(value, QUAD, pairs)  13.8 us
    all_to_all x1, blocking collectives, local(): spread = lax.all_to_all(spread, BAND, 0, 0)  12.3 us
    ppermute x1, starting transfers between devices, local(): lax.ppermute(outgoing, ('z1', 'z0'), [(0, 2), (3, 1), (2, 3), (1, 0)])  11.7 us
    all_to_all x1, blocking collectives, local(): lax.all_to_all(call(far_kernel, f32(8, 24, 128), near, own, onward), FAR,...  10.9 us
    all_to_all x1, blocking collectives, local(): near = lax.all_to_all(to_quad, QUAD, 0, 0)  10.3 us
    all_to_all x1, blocking collectives, local(): lax.all_to_all(call(pack_kernel, f32(16, 24, 128), near, itself, far), BA...  10.3 us
    pallas_call x6, Pallas kernels, call(): pl.pallas_call(kernel, scratch_shapes=scratch, cost_estimate=cost, out_sh...  6.05 us
    pallas_call x3, Pallas kernels, cut(): pl.pallas_call(functools.partial(cut_kernel, pieces), out_shape=tuple((f3...  4.01 us
  transfers between devices with their start and end apart: 5, of which 1 were waited for; matrix products, arithmetic and copies ran while one was open for 0% of the time, Pallas kernels for 9%

profile of v5, /device:TPU:1, one launch (start us, length us, event | category | flops | bytes accessed | tf_op | source)
XLA Modules:
  0.0 82.5 jit_solution(11660138615707387200)
XLA Ops:
  0.0 1.4 %shard_map.17 = (f32[2,64,2048]{2,1,0:T(8,128)S(1)}, f32[2,64,1024]{2,1,0:T(8,128)S(1)}) custom-call(f32[2,64,4096]{2,1,0:T(8,128)} %templates_ref.4), custom_call_target="tpu_custom_call" | custom-call | tf_op jit(solution)/shard_map/pallas_call | solution.py:90
  1.4 0.7 collective-permute-start.3
  2.1 9.7 %collective-permute-start = (f32[2,64,1024]{2,1,0:T(8,128)S(1)}, f32[2,64,1024]{2,1,0:T(8,128)S(1)}, u32[]{:S(2)}, u32[]{:S(2)}) collective-permute-start(f32[2,64,1024]{2,1,0:T(8,128)S(1)} %get-tuple-element.28), channel_id=1, source_target_pairs={{0,3},{1,2},{2,1},{3,0},{4,7},{5,6},{6,5},{7,4},{8,11},{9,10},{10,... | collective-permute-start | bytes 1572872 | tf_op jit(solution)/shard_map/ppermute | solution.py:239
  11.8 1.4 %shard_map.18 = (f32[2,64,1024]{2,1,0:T(8,128)S(1)}, f32[2,64,1024]{2,1,0:T(8,128)S(1)}, f32[2,64,1024]{2,1,0:T(8,128)S(1)}) custom-call(f32[2,64,4096]{2,1,0:T(8,128)} %templates_ref.4), custom_call_target="tpu_custom_call" | custom-call | tf_op jit(solution)/shard_map/pallas_call | solution.py:90
  13.2 2.1 %collective-permute-start.1 = (f32[2,64,1024]{2,1,0:T(8,128)S(1)}, f32[2,64,1024]{2,1,0:T(8,128)S(1)}, u32[]{:S(2)}, u32[]{:S(2)}) collective-permute-start(f32[2,64,1024]{2,1,0:T(8,128)S(1)} %get-tuple-element.35), channel_id=1, source_target_pairs={{0,1},{1,0},{2,3},{3,2},{4,5},{5,4},{6,7},{7,6},{8,9},{9,8},{10,11... | collective-permute-start | bytes 1572872 | tf_op jit(solution)/shard_map/ppermute | solution.py:239
  15.3 2.0 %collective-permute-start.2 = (f32[2,64,1024]{2,1,0:T(8,128)S(1)}, f32[2,64,1024]{2,1,0:T(8,128)S(1)}, u32[]{:S(2)}, u32[]{:S(2)}) collective-permute-start(f32[2,64,1024]{2,1,0:T(8,128)S(1)} %get-tuple-element.30), channel_id=1, source_target_pairs={{0,2},{1,3},{2,0},{3,1},{4,6},{5,7},{6,4},{7,5},{8,10},{9,11},{10,... | collective-permute-start | bytes 1572872 | tf_op jit(solution)/shard_map/ppermute | solution.py:239
  17.3 1.2 %shard_map.19.second_ref = f32[2,64,2048]{2,1,0:T(8,128)S(1)} custom-call(f32[2,64,4096]{2,1,0:T(8,128)} %templates_ref.4), custom_call_target="tpu_custom_call" | custom-call | tf_op jit(solution)/shard_map/pallas_call | solution.py:90
  18.6 2.8 %shard_map.20 = (bf16[256,2048]{1,0:T(8,128)(2,1)S(1)}, f32[16,8,128]{2,1,0:T(8,128)S(1)}) custom-call(f32[2,64,4096]{2,1,0:T(8,128)} %templates_ref.4), custom_call_target="tpu_custom_call" | custom-call | tf_op jit(solution)/shard_map/pallas_call | solution.py:21
  21.3 0.0 collective-permute-done.3.passing_ref
  21.4 0.1 shard_map.21
  21.5 11.7 %collective-permute-start.4 = (f32[2,64,2048]{2,1,0:T(8,128)S(1)}, f32[2,64,2048]{2,1,0:T(8,128)S(1)}, u32[]{:S(2)}, u32[]{:S(2)}) collective-permute-start(f32[2,64,2048]{2,1,0:T(8,128)S(1)} %shard_map.21), channel_id=1, source_target_pairs={{0,4},{6,2},{4,6},{2,0},{1,5},{7,3},{5,7},{3,1},{8,12},{14,10},{12... | collective-permute-start | bytes 3145736 | tf_op jit(solution)/shard_map/ppermute | solution.py:256
  33.1 0.0 collective-permute-done.three_ref
  33.1 2.2 %collective-permute-done.1.one_ref = f32[2,64,1024]{2,1,0:T(8,128)S(1)} collective-permute-done((f32[2,64,1024]{2,1,0:T(8,128)S(1)}, f32[2,64,1024]{2,1,0:T(8,128)S(1)}, u32[]{:S(2)}, u32[]{:S(2)}) %collective-permute-start.1) | collective-permute-done | bytes 524320 | tf_op jit(solution)/shard_map/ppermute | solution.py:239
  35.4 0.0 collective-permute-done.2.two_ref
  35.4 1.6 %shard_map.22 = f32[16,32,128]{2,1,0:T(8,128)S(1)} custom-call(f32[16,8,128]{2,1,0:T(8,128)S(1)} %get-tuple-element.33.itself_ref, f32[2,64,1024]{2,1,0:T(8,128)S(1)} %get-tuple-element.42.own_ref, f32[2,64,1024]{2,1,0:T(8,128)S(1)} %collective-permute-done.three_ref, f32[2,64,1024]{2,1,0:T(8,128)S(1)} %collective-permute-done.1.one_ref, ...), custom_call_target="tpu_custom_call" | custom-call | flops 46000001024 | bytes 4194304 | tf_op jit(solution)/shard_map/pallas_call | solution.py:21
  37.0 12.3 %all_to_all.20.spread_ref = f32[16,32,128]{2,1,0:T(8,128)S(1)} all-to-all(f32[16,32,128]{2,1,0:T(8,128)S(1)} %shard_map.22), channel_id=1, replica_groups=mesh['y'=4,'x_lo'=2,'core'=2,'z_hi'=4,'z1'=2,'z0'=2,'x_hi'=2] {'y','x_lo..., dimensions={0} | all-to-all | bytes 524288 | tf_op jit(solution)/shard_map/all_to_all | solution.py:262
  49.3 10.3 %all_to_all.21.near_ref = f32[4,16,128]{2,1,0:T(8,128)S(1)} all-to-all(f32[4,16,128]{2,1,0:T(8,128)S(1)} %get-tuple-element.46), channel_id=1, replica_groups=mesh['y'=4,'x_lo'=2,'core'=2,'z_hi'=4,'z1'=2,'z0'=2,'x_hi'=2] {'z0','x_hi'}, dimensions={0} | all-to-all | bytes 65536 | tf_op jit(solution)/shard_map/all_to_all | solution.py:264
  59.6 0.0 collective-permute-done.4.far_ref
  59.6 0.6 shard_map.24
  60.3 10.9 %all_to_all.22.far_ref = f32[8,24,128]{2,1,0:T(8,128)S(1)} all-to-all(f32[8,24,128]{2,1,0:T(8,128)S(1)} %shard_map.24), channel_id=1, replica_groups=mesh['y'=4,'x_lo'=2,'core'=2,'z_hi'=4,'z1'=2,'z0'=2,'x_hi'=2] {'z1','x_l..., dimensions={0} | all-to-all | bytes 196608 | tf_op jit(solution)/shard_map/all_to_all | solution.py:266
  71.2 0.2 shard_map.25
  71.4 10.3 %all_to_all.23.shares_ref = f32[16,24,128]{2,1,0:T(8,128)S(1)} all-to-all(f32[16,24,128]{2,1,0:T(8,128)S(1)} %shard_map.25), channel_id=1, replica_groups=mesh['y'=4,'x_lo'=2,'core'=2,'z_hi'=4,'z1'=2,'z0'=2,'x_hi'=2] {'y','x_lo..., dimensions={0} | all-to-all | bytes 393216 | tf_op jit(solution)/shard_map/all_to_all | solution.py:267
  81.6 0.9 %shard_map.26 = f32[5,64,64]{2,1,0:T(8,128)} custom-call(f32[4,16,128]{2,1,0:T(8,128)S(1)} %all_to_all.21.near_ref, f32[8,24,128]{2,1,0:T(8,128)S(1)} %all_to_all.22.far_ref, f32[16,24,128]{2,1,0:T(8,128)S(1)} %all_to_all.23.shares_ref), custom_call_target="tpu_custom_call" | custom-call | tf_op jit(solution)/shard_map/pallas_call | solution.py:21
  (1 shorter events, 0.0 us)
Async XLA Ops:
  1.4 20.0 %collective-permute-start.3 = (f32[2,64,2048]{2,1,0:T(8,128)S(1)}, f32[2,64,2048]{2,1,0:T(8,128)S(1)}, u32[]{:S(2)}, u32[]{:S(2)}) collective-permute-start(f32[2,64,2048]{2,1,0:T(8,128)S(1)} %get-tuple-element.37), channel_id=1, source_target_pairs={{2,4},{4,2},{3,5},{5,3},{10,12},{12,10},{11,13},{13,11},{18,20},{2... | collective-permute-start | bytes 3145736 | tf_op jit(solution)/shard_map/ppermute | solution.py:245
  2.1 31.0 %collective-permute-start = (f32[2,64,1024]{2,1,0:T(8,128)S(1)}, f32[2,64,1024]{2,1,0:T(8,128)S(1)}, u32[]{:S(2)}, u32[]{:S(2)}) collective-permute-start(f32[2,64,1024]{2,1,0:T(8,128)S(1)} %get-tuple-element.28), channel_id=1, source_target_pairs={{0,3},{1,2},{2,1},{3,0},{4,7},{5,6},{6,5},{7,4},{8,11},{9,10},{10,... | collective-permute-start | bytes 1572872 | tf_op jit(solution)/shard_map/ppermute | solution.py:239
  13.2 22.2 %collective-permute-start.1 = (f32[2,64,1024]{2,1,0:T(8,128)S(1)}, f32[2,64,1024]{2,1,0:T(8,128)S(1)}, u32[]{:S(2)}, u32[]{:S(2)}) collective-permute-start(f32[2,64,1024]{2,1,0:T(8,128)S(1)} %get-tuple-element.35), channel_id=1, source_target_pairs={{0,1},{1,0},{2,3},{3,2},{4,5},{5,4},{6,7},{7,6},{8,9},{9,8},{10,11... | collective-permute-start | bytes 1572872 | tf_op jit(solution)/shard_map/ppermute | solution.py:239
  15.3 20.1 %collective-permute-start.2 = (f32[2,64,1024]{2,1,0:T(8,128)S(1)}, f32[2,64,1024]{2,1,0:T(8,128)S(1)}, u32[]{:S(2)}, u32[]{:S(2)}) collective-permute-start(f32[2,64,1024]{2,1,0:T(8,128)S(1)} %get-tuple-element.30), channel_id=1, source_target_pairs={{0,2},{1,3},{2,0},{3,1},{4,6},{5,7},{6,4},{7,5},{8,10},{9,11},{10,... | collective-permute-start | bytes 1572872 | tf_op jit(solution)/shard_map/ppermute | solution.py:239
  21.5 38.2 %collective-permute-start.4 = (f32[2,64,2048]{2,1,0:T(8,128)S(1)}, f32[2,64,2048]{2,1,0:T(8,128)S(1)}, u32[]{:S(2)}, u32[]{:S(2)}) collective-permute-start(f32[2,64,2048]{2,1,0:T(8,128)S(1)} %shard_map.21), channel_id=1, source_target_pairs={{0,4},{6,2},{4,6},{2,0},{1,5},{7,3},{5,7},{3,1},{8,12},{14,10},{12... | collective-permute-start | bytes 3145736 | tf_op jit(solution)/shard_map/ppermute | solution.py:256

commit v6 on v5

--- a/solution.py
+++ b/solution.py
@@ -245,10 +245,11 @@
     passing = lax.ppermute(first, ("z1", "z0"), [(1, 2), (2, 1)])
     three = swapped(third, 3)
     third, templates = lax.optimization_barrier((third, templates))
-    other, nearest, mine = cut(templates, ("quarter", 2), ("quarter", 1), ("quarter", 0))
-    blocks = [mine, three, swapped(nearest, 1), swapped(other, 2)]
+    other, mine = cut(templates, ("quarter", 2), ("quarter", 0))
+    two = swapped(other, 2)
     other, templates = lax.optimization_barrier((other, templates))
-    (second,) = cut(templates, ("half", 1))
+    nearest, second = cut(templates, ("quarter", 1), ("half", 1))
+    blocks = [mine, three, swapped(nearest, 1), two]
     second, templates = lax.optimization_barrier((second, templates))
     own, shares = call(own_kernel, (jax.ShapeDtypeStruct((256, 2048), jnp.bfloat16), f32(16, 8, 128)), templates)
     second, passing, own = lax.optimization_barrier((second, passing, own))

time: 82.9 us -> 82.9 us (level)
  transfers between devices with their start and end apart: 5 -> 5, of which waited for: 1 -> 2; matrix products, arithmetic and copies ran while one was open for 0% -> 0% of each run, Pallas kernels for 9% -> 9%
where the time goes in v6:
time: 82.9 us; the launch traced here: 82.5 us
  blocking collectives  43.7 us (53%)
  starting transfers between devices  26.1 us (31%)
  Pallas kernels  10.2 us (12%)
  waiting for transfers between devices  2.31 us (3%)
    ppermute x3, starting transfers between devices, swapped(): return lax.ppermute(value, QUAD, pairs)  13.8 us
    all_to_all x1, blocking collectives, local(): spread = lax.all_to_all(spread, BAND, 0, 0)  12.3 us
    ppermute x1, starting transfers between devices, local(): lax.ppermute(outgoing, ('z1', 'z0'), [(0, 2), (3, 1), (2, 3), (1, 0)])  11.6 us
    all_to_all x1, blocking collectives, local(): lax.all_to_all(call(far_kernel, f32(8, 24, 128), near, own, onward), FAR,...  10.9 us
    all_to_all x1, blocking collectives, local(): near = lax.all_to_all(to_quad, QUAD, 0, 0)  10.3 us
    all_to_all x1, blocking collectives, local(): lax.all_to_all(call(pack_kernel, f32(16, 24, 128), near, itself, far), BA...  10.3 us
    pallas_call x6, Pallas kernels, call(): pl.pallas_call(kernel, scratch_shapes=scratch, cost_estimate=cost, out_sh...  6.06 us
    pallas_call x3, Pallas kernels, cut(): pl.pallas_call(functools.partial(cut_kernel, pieces), out_shape=tuple((f3...  4.02 us
  transfers between devices with their start and end apart: 5, of which 2 were waited for; matrix products, arithmetic and copies ran while one was open for 0% of the time, Pallas kernels for 9%

profile of v6, /device:TPU:1, one launch (start us, length us, event | category | flops | bytes accessed | tf_op | source)
XLA Modules:
  0.0 82.5 jit_solution(17334231639648701355)
XLA Ops:
  0.0 1.4 %shard_map.17 = (f32[2,64,2048]{2,1,0:T(8,128)S(1)}, f32[2,64,1024]{2,1,0:T(8,128)S(1)}) custom-call(f32[2,64,4096]{2,1,0:T(8,128)} %templates_ref.4), custom_call_target="tpu_custom_call" | custom-call | tf_op jit(solution)/shard_map/pallas_call | solution.py:90
  1.4 0.7 collective-permute-start.3
  2.1 9.7 %collective-permute-start = (f32[2,64,1024]{2,1,0:T(8,128)S(1)}, f32[2,64,1024]{2,1,0:T(8,128)S(1)}, u32[]{:S(2)}, u32[]{:S(2)}) collective-permute-start(f32[2,64,1024]{2,1,0:T(8,128)S(1)} %get-tuple-element.29), channel_id=1, source_target_pairs={{0,3},{1,2},{2,1},{3,0},{4,7},{5,6},{6,5},{7,4},{8,11},{9,10},{10,... | collective-permute-start | bytes 1572872 | tf_op jit(solution)/shard_map/ppermute | solution.py:239
  11.8 1.2 %shard_map.18 = (f32[2,64,1024]{2,1,0:T(8,128)S(1)}, f32[2,64,1024]{2,1,0:T(8,128)S(1)}) custom-call(f32[2,64,4096]{2,1,0:T(8,128)} %templates_ref.4), custom_call_target="tpu_custom_call" | custom-call | tf_op jit(solution)/shard_map/pallas_call | solution.py:90
  13.0 1.9 %collective-permute-start.2 = (f32[2,64,1024]{2,1,0:T(8,128)S(1)}, f32[2,64,1024]{2,1,0:T(8,128)S(1)}, u32[]{:S(2)}, u32[]{:S(2)}) collective-permute-start(f32[2,64,1024]{2,1,0:T(8,128)S(1)} %get-tuple-element.31), channel_id=1, source_target_pairs={{0,2},{1,3},{2,0},{3,1},{4,6},{5,7},{6,4},{7,5},{8,10},{9,11},{10,... | collective-permute-start | bytes 1572872 | tf_op jit(solution)/shard_map/ppermute | solution.py:239
  14.9 1.4 %shard_map.19 = (f32[2,64,1024]{2,1,0:T(8,128)S(1)}, f32[2,64,2048]{2,1,0:T(8,128)S(1)}) custom-call(f32[2,64,4096]{2,1,0:T(8,128)} %templates_ref.4), custom_call_target="tpu_custom_call" | custom-call | tf_op jit(solution)/shard_map/pallas_call | solution.py:90
  16.4 2.2 %collective-permute-start.1 = (f32[2,64,1024]{2,1,0:T(8,128)S(1)}, f32[2,64,1024]{2,1,0:T(8,128)S(1)}, u32[]{:S(2)}, u32[]{:S(2)}) collective-permute-start(f32[2,64,1024]{2,1,0:T(8,128)S(1)} %get-tuple-element.37), channel_id=1, source_target_pairs={{0,1},{1,0},{2,3},{3,2},{4,5},{5,4},{6,7},{7,6},{8,9},{9,8},{10,11... | collective-permute-start | bytes 1572872 | tf_op jit(solution)/shard_map/ppermute | solution.py:239
  18.6 2.8 %shard_map.20 = (bf16[256,2048]{1,0:T(8,128)(2,1)S(1)}, f32[16,8,128]{2,1,0:T(8,128)S(1)}) custom-call(f32[2,64,4096]{2,1,0:T(8,128)} %templates_ref.4), custom_call_target="tpu_custom_call" | custom-call | tf_op jit(solution)/shard_map/pallas_call | solution.py:21
  21.4 0.0 collective-permute-done.3.passing_ref
  21.4 0.1 shard_map.21
  21.5 11.6 %collective-permute-start.4 = (f32[2,64,2048]{2,1,0:T(8,128)S(1)}, f32[2,64,2048]{2,1,0:T(8,128)S(1)}, u32[]{:S(2)}, u32[]{:S(2)}) collective-permute-start(f32[2,64,2048]{2,1,0:T(8,128)S(1)} %shard_map.21), channel_id=1, source_target_pairs={{0,4},{6,2},{4,6},{2,0},{1,5},{7,3},{5,7},{3,1},{8,12},{14,10},{12... | collective-permute-start | bytes 3145736 | tf_op jit(solution)/shard_map/ppermute | solution.py:257
  33.1 0.0 collective-permute-done.three_ref
  33.1 0.2 collective-permute-done.2.two_ref
  33.3 2.1 %collective-permute-done.1.one_ref = f32[2,64,1024]{2,1,0:T(8,128)S(1)} collective-permute-done((f32[2,64,1024]{2,1,0:T(8,128)S(1)}, f32[2,64,1024]{2,1,0:T(8,128)S(1)}, u32[]{:S(2)}, u32[]{:S(2)}) %collective-permute-start.1) | collective-permute-done | bytes 524320 | tf_op jit(solution)/shard_map/ppermute | solution.py:239
  35.4 1.6 %shard_map.22 = f32[16,32,128]{2,1,0:T(8,128)S(1)} custom-call(f32[16,8,128]{2,1,0:T(8,128)S(1)} %get-tuple-element.35.itself_ref, f32[2,64,1024]{2,1,0:T(8,128)S(1)} %get-tuple-element.44.own_ref, f32[2,64,1024]{2,1,0:T(8,128)S(1)} %collective-permute-done.three_ref, f32[2,64,1024]{2,1,0:T(8,128)S(1)} %collective-permute-done.1.one_ref, ...), custom_call_target="tpu_custom_call" | custom-call | flops 46000001024 | bytes 4194304 | tf_op jit(solution)/shard_map/pallas_call | solution.py:21
  37.0 12.3 %all_to_all.20.spread_ref = f32[16,32,128]{2,1,0:T(8,128)S(1)} all-to-all(f32[16,32,128]{2,1,0:T(8,128)S(1)} %shard_map.22), channel_id=1, replica_groups=mesh['y'=4,'x_lo'=2,'core'=2,'z_hi'=4,'z1'=2,'z0'=2,'x_hi'=2] {'y','x_lo..., dimensions={0} | all-to-all | bytes 524288 | tf_op jit(solution)/shard_map/all_to_all | solution.py:263
  49.3 10.3 %all_to_all.21.near_ref = f32[4,16,128]{2,1,0:T(8,128)S(1)} all-to-all(f32[4,16,128]{2,1,0:T(8,128)S(1)} %get-tuple-element.48), channel_id=1, replica_groups=mesh['y'=4,'x_lo'=2,'core'=2,'z_hi'=4,'z1'=2,'z0'=2,'x_hi'=2] {'z0','x_hi'}, dimensions={0} | all-to-all | bytes 65536 | tf_op jit(solution)/shard_map/all_to_all | solution.py:265
  59.6 0.0 collective-permute-done.4.far_ref
  59.6 0.6 shard_map.24
  60.3 10.9 %all_to_all.22.far_ref = f32[8,24,128]{2,1,0:T(8,128)S(1)} all-to-all(f32[8,24,128]{2,1,0:T(8,128)S(1)} %shard_map.24), channel_id=1, replica_groups=mesh['y'=4,'x_lo'=2,'core'=2,'z_hi'=4,'z1'=2,'z0'=2,'x_hi'=2] {'z1','x_l..., dimensions={0} | all-to-all | bytes 196608 | tf_op jit(solution)/shard_map/all_to_all | solution.py:267
  71.2 0.2 shard_map.25
  71.3 10.3 %all_to_all.23.shares_ref = f32[16,24,128]{2,1,0:T(8,128)S(1)} all-to-all(f32[16,24,128]{2,1,0:T(8,128)S(1)} %shard_map.25), channel_id=1, replica_groups=mesh['y'=4,'x_lo'=2,'core'=2,'z_hi'=4,'z1'=2,'z0'=2,'x_hi'=2] {'y','x_lo..., dimensions={0} | all-to-all | bytes 393216 | tf_op jit(solution)/shard_map/all_to_all | solution.py:268
  81.6 0.9 %shard_map.26 = f32[5,64,64]{2,1,0:T(8,128)} custom-call(f32[4,16,128]{2,1,0:T(8,128)S(1)} %all_to_all.21.near_ref, f32[8,24,128]{2,1,0:T(8,128)S(1)} %all_to_all.22.far_ref, f32[16,24,128]{2,1,0:T(8,128)S(1)} %all_to_all.23.shares_ref), custom_call_target="tpu_custom_call" | custom-call | tf_op jit(solution)/shard_map/pallas_call | solution.py:21
  (1 shorter events, 0.0 us)
Async XLA Ops:
  1.4 20.0 %collective-permute-start.3 = (f32[2,64,2048]{2,1,0:T(8,128)S(1)}, f32[2,64,2048]{2,1,0:T(8,128)S(1)}, u32[]{:S(2)}, u32[]{:S(2)}) collective-permute-start(f32[2,64,2048]{2,1,0:T(8,128)S(1)} %get-tuple-element.39), channel_id=1, source_target_pairs={{2,4},{4,2},{3,5},{5,3},{10,12},{12,10},{11,13},{13,11},{18,20},{2... | collective-permute-start | bytes 3145736 | tf_op jit(solution)/shard_map/ppermute | solution.py:245
  2.1 31.0 %collective-permute-start = (f32[2,64,1024]{2,1,0:T(8,128)S(1)}, f32[2,64,1024]{2,1,0:T(8,128)S(1)}, u32[]{:S(2)}, u32[]{:S(2)}) collective-permute-start(f32[2,64,1024]{2,1,0:T(8,128)S(1)} %get-tuple-element.29), channel_id=1, source_target_pairs={{0,3},{1,2},{2,1},{3,0},{4,7},{5,6},{6,5},{7,4},{8,11},{9,10},{10,... | collective-permute-start | bytes 1572872 | tf_op jit(solution)/shard_map/ppermute | solution.py:239
  13.0 20.3 %collective-permute-start.2 = (f32[2,64,1024]{2,1,0:T(8,128)S(1)}, f32[2,64,1024]{2,1,0:T(8,128)S(1)}, u32[]{:S(2)}, u32[]{:S(2)}) collective-permute-start(f32[2,64,1024]{2,1,0:T(8,128)S(1)} %get-tuple-element.31), channel_id=1, source_target_pairs={{0,2},{1,3},{2,0},{3,1},{4,6},{5,7},{6,4},{7,5},{8,10},{9,11},{10,... | collective-permute-start | bytes 1572872 | tf_op jit(solution)/shard_map/ppermute | solution.py:239
  16.4 19.1 %collective-permute-start.1 = (f32[2,64,1024]{2,1,0:T(8,128)S(1)}, f32[2,64,1024]{2,1,0:T(8,128)S(1)}, u32[]{:S(2)}, u32[]{:S(2)}) collective-permute-start(f32[2,64,1024]{2,1,0:T(8,128)S(1)} %get-tuple-element.37), channel_id=1, source_target_pairs={{0,1},{1,0},{2,3},{3,2},{4,5},{5,4},{6,7},{7,6},{8,9},{9,8},{10,11... | collective-permute-start | bytes 1572872 | tf_op jit(solution)/shard_map/ppermute | solution.py:239
  21.5 38.1 %collective-permute-start.4 = (f32[2,64,2048]{2,1,0:T(8,128)S(1)}, f32[2,64,2048]{2,1,0:T(8,128)S(1)}, u32[]{:S(2)}, u32[]{:S(2)}) collective-permute-start(f32[2,64,2048]{2,1,0:T(8,128)S(1)} %shard_map.21), channel_id=1, source_target_pairs={{0,4},{6,2},{4,6},{2,0},{1,5},{7,3},{5,7},{3,1},{8,12},{14,10},{12... | collective-permute-start | bytes 3145736 | tf_op jit(solution)/shard_map/ppermute | solution.py:257

commit v7 on v5

--- a/solution.py
+++ b/solution.py
@@ -129,9 +129,11 @@
     return (member_index() & (1 if k == 1 else 2)) != 0
 
 
-def own_kernel(templates_ref, own_ref, shares_ref):
+def own_kernel(templates_ref, own_ref, shares_ref, mine_ref):
     at = pl.multiple_of(jnp.where(is_middle(), 2048, 0), 2048)
     own_ref[...] = jnp.concatenate(split(templates_ref[:, :, pl.ds(at, 2048)].reshape(128, 2048)), axis=0)
+    at = pl.multiple_of(member_index() * 1024, 1024)
+    mine_ref[...] = jnp.concatenate(split(templates_ref[:, :, pl.ds(at, 1024)].reshape(128, 1024)), axis=0)
     rows = jnp.concatenate(split(templates_ref[...].reshape(128, 4096)), axis=0)
     tile = complex_tile(four_passes(dot(rows, rows)))
     row = lax.broadcasted_iota(jnp.int32, (64, 128), 0)
@@ -144,7 +146,9 @@
 
 
 def near_kernel(itself_ref, own_ref, three_ref, one_ref, two_ref, out_ref, high_ref, low_ref):
-    for offset, ref in enumerate((own_ref, one_ref, two_ref, three_ref)):
+    high_ref[member_index()] = own_ref[:128, :]
+    low_ref[member_index()] = own_ref[128:, :]
+    for offset, ref in ((1, one_ref), (2, two_ref), (3, three_ref)):
         high, low = split(ref[...].reshape(128, 1024))
         high_ref[member_index() ^ offset] = high
         low_ref[member_index() ^ offset] = low
@@ -245,12 +249,13 @@
     passing = lax.ppermute(first, ("z1", "z0"), [(1, 2), (2, 1)])
     three = swapped(third, 3)
     third, templates = lax.optimization_barrier((third, templates))
-    other, nearest, mine = cut(templates, ("quarter", 2), ("quarter", 1), ("quarter", 0))
-    blocks = [mine, three, swapped(nearest, 1), swapped(other, 2)]
+    other, nearest = cut(templates, ("quarter", 2), ("quarter", 1))
+    blocks = [three, swapped(nearest, 1), swapped(other, 2)]
     other, templates = lax.optimization_barrier((other, templates))
     (second,) = cut(templates, ("half", 1))
     second, templates = lax.optimization_barrier((second, templates))
-    own, shares = call(own_kernel, (jax.ShapeDtypeStruct((256, 2048), jnp.bfloat16), f32(16, 8, 128)), templates)
+    halves = [jax.ShapeDtypeStruct((256, size), jnp.bfloat16) for size in (2048, 1024)]
+    own, shares, mine = call(own_kernel, (halves[0], f32(16, 8, 128), halves[1]), templates)
     second, passing, own = lax.optimization_barrier((second, passing, own))
     outgoing = choose(second, passing)
     onward = lax.ppermute(outgoing, ("z1", "z0"), [(0, 2), (3, 1), (2, 3), (1, 0)])
@@ -258,7 +263,7 @@
     blocks, own, outgoing = lax.optimization_barrier((blocks, own, outgoing))
     cost = pl.CostEstimate(flops=46 * 10**9, bytes_accessed=4 * 2**20, transcendentals=0)
     terms = (pltpu.VMEM((4, 128, 1024), jnp.bfloat16),) * 2
-    spread = call(near_kernel, f32(16, 32, 128), shares, *blocks, cost=cost, scratch=terms)
+    spread = call(near_kernel, f32(16, 32, 128), shares, mine, *blocks, cost=cost, scratch=terms)
     spread = lax.all_to_all(spread, BAND, 0, 0)
     to_quad, itself = call(sum_kernel, (f32(4, 16, 128), f32(8, 128)), spread)
     near = lax.all_to_all(to_quad, QUAD, 0, 0)

time: 82.9 us -> 82.9 us (level)
  no operation moved by 1% of the time
where the time goes in v7:
time: 82.9 us; the launch traced here: 82.5 us
  blocking collectives  43.9 us (53%)
  starting transfers between devices  26.1 us (31%)
  Pallas kernels  10.1 us (12%)
  waiting for transfers between devices  2.25 us (3%)
    ppermute x3, starting transfers between devices, swapped(): return lax.ppermute(value, QUAD, pairs)  13.8 us
    all_to_all x1, blocking collectives, local(): spread = lax.all_to_all(spread, BAND, 0, 0)  12.3 us
    ppermute x1, starting transfers between devices, local(): lax.ppermute(outgoing, ('z1', 'z0'), [(0, 2), (3, 1), (2, 3), (1, 0)])  11.6 us
    all_to_all x1, blocking collectives, local(): lax.all_to_all(call(far_kernel, f32(8, 24, 128), near, own, onward), FAR,...  10.9 us
    all_to_all x1, blocking collectives, local(): lax.all_to_all(call(pack_kernel, f32(16, 24, 128), near, itself, far), BA...  10.4 us
    all_to_all x1, blocking collectives, local(): near = lax.all_to_all(to_quad, QUAD, 0, 0)  10.3 us
    pallas_call x6, Pallas kernels, call(): pl.pallas_call(kernel, scratch_shapes=scratch, cost_estimate=cost, out_sh...  6.11 us
    pallas_call x3, Pallas kernels, cut(): pl.pallas_call(functools.partial(cut_kernel, pieces), out_shape=tuple((f3...  3.84 us
  transfers between devices with their start and end apart: 5, of which 1 were waited for; matrix products, arithmetic and copies ran while one was open for 0% of the time, Pallas kernels for 9%

profile of v7, /device:TPU:1, one launch (start us, length us, event | category | flops | bytes accessed | tf_op | source)
XLA Modules:
  0.0 82.5 jit_solution(1098749537506081807)
XLA Ops:
  0.0 1.4 %shard_map.17 = (f32[2,64,2048]{2,1,0:T(8,128)S(1)}, f32[2,64,1024]{2,1,0:T(8,128)S(1)}) custom-call(f32[2,64,4096]{2,1,0:T(8,128)} %templates_ref.4), custom_call_target="tpu_custom_call" | custom-call | tf_op jit(solution)/shard_map/pallas_call | solution.py:90
  1.4 0.7 collective-permute-start.3
  2.1 9.7 %collective-permute-start = (f32[2,64,1024]{2,1,0:T(8,128)S(1)}, f32[2,64,1024]{2,1,0:T(8,128)S(1)}, u32[]{:S(2)}, u32[]{:S(2)}) collective-permute-start(f32[2,64,1024]{2,1,0:T(8,128)S(1)} %get-tuple-element.27), channel_id=1, source_target_pairs={{0,3},{1,2},{2,1},{3,0},{4,7},{5,6},{6,5},{7,4},{8,11},{9,10},{10,... | collective-permute-start | bytes 1572872 | tf_op jit(solution)/shard_map/ppermute | solution.py:243
  11.8 1.2 %shard_map.18 = (f32[2,64,1024]{2,1,0:T(8,128)S(1)}, f32[2,64,1024]{2,1,0:T(8,128)S(1)}) custom-call(f32[2,64,4096]{2,1,0:T(8,128)} %templates_ref.4), custom_call_target="tpu_custom_call" | custom-call | tf_op jit(solution)/shard_map/pallas_call | solution.py:90
  13.0 2.1 %collective-permute-start.1 = (f32[2,64,1024]{2,1,0:T(8,128)S(1)}, f32[2,64,1024]{2,1,0:T(8,128)S(1)}, u32[]{:S(2)}, u32[]{:S(2)}) collective-permute-start(f32[2,64,1024]{2,1,0:T(8,128)S(1)} %get-tuple-element.34), channel_id=1, source_target_pairs={{0,1},{1,0},{2,3},{3,2},{4,5},{5,4},{6,7},{7,6},{8,9},{9,8},{10,11... | collective-permute-start | bytes 1572872 | tf_op jit(solution)/shard_map/ppermute | solution.py:243
  15.2 2.0 %collective-permute-start.2 = (f32[2,64,1024]{2,1,0:T(8,128)S(1)}, f32[2,64,1024]{2,1,0:T(8,128)S(1)}, u32[]{:S(2)}, u32[]{:S(2)}) collective-permute-start(f32[2,64,1024]{2,1,0:T(8,128)S(1)} %get-tuple-element.29), channel_id=1, source_target_pairs={{0,2},{1,3},{2,0},{3,1},{4,6},{5,7},{6,4},{7,5},{8,10},{9,11},{10,... | collective-permute-start | bytes 1572872 | tf_op jit(solution)/shard_map/ppermute | solution.py:243
  17.1 1.2 %shard_map.19.second_ref = f32[2,64,2048]{2,1,0:T(8,128)S(1)} custom-call(f32[2,64,4096]{2,1,0:T(8,128)} %templates_ref.4), custom_call_target="tpu_custom_call" | custom-call | tf_op jit(solution)/shard_map/pallas_call | solution.py:90
  18.4 3.0 %shard_map.20 = (bf16[256,2048]{1,0:T(8,128)(2,1)S(1)}, f32[16,8,128]{2,1,0:T(8,128)S(1)}, bf16[256,1024]{1,0:T(8,128)(2,1)S(1)}) custom-call(f32[2,64,4096]{2,1,0:T(8,128)} %templates_ref.4), custom_call_target="tpu_custom_call" | custom-call | tf_op jit(solution)/shard_map/pallas_call | solution.py:21
  21.4 0.0 collective-permute-done.3.passing_ref
  21.4 0.1 shard_map.21
  21.5 11.6 %collective-permute-start.4 = (f32[2,64,2048]{2,1,0:T(8,128)S(1)}, f32[2,64,2048]{2,1,0:T(8,128)S(1)}, u32[]{:S(2)}, u32[]{:S(2)}) collective-permute-start(f32[2,64,2048]{2,1,0:T(8,128)S(1)} %shard_map.21), channel_id=1, source_target_pairs={{0,4},{6,2},{4,6},{2,0},{1,5},{7,3},{5,7},{3,1},{8,12},{14,10},{12... | collective-permute-start | bytes 3145736 | tf_op jit(solution)/shard_map/ppermute | solution.py:261
  33.1 0.0 collective-permute-done.three_ref
  33.1 2.2 %collective-permute-done.1.one_ref = f32[2,64,1024]{2,1,0:T(8,128)S(1)} collective-permute-done((f32[2,64,1024]{2,1,0:T(8,128)S(1)}, f32[2,64,1024]{2,1,0:T(8,128)S(1)}, u32[]{:S(2)}, u32[]{:S(2)}) %collective-permute-start.1) | collective-permute-done | bytes 524320 | tf_op jit(solution)/shard_map/ppermute | solution.py:243
  35.4 0.0 collective-permute-done.2.two_ref
  35.4 1.5 %shard_map.22 = f32[16,32,128]{2,1,0:T(8,128)S(1)} custom-call(f32[16,8,128]{2,1,0:T(8,128)S(1)} %get-tuple-element.32.itself_ref, bf16[256,1024]{1,0:T(8,128)(2,1)S(1)} %get-tuple-element.33.own_ref, f32[2,64,1024]{2,1,0:T(8,128)S(1)} %collective-permute-done.three_ref, f32[2,64,1024]{2,1,0:T(8,128)S(1)} %collective-permute-done.1.one_ref, ...), custom_call_target="tpu_custom_call" | custom-call | flops 46000001024 | bytes 4194304 | tf_op jit(solution)/shard_map/pallas_call | solution.py:21
  36.9 12.3 %all_to_all.20.spread_ref = f32[16,32,128]{2,1,0:T(8,128)S(1)} all-to-all(f32[16,32,128]{2,1,0:T(8,128)S(1)} %shard_map.22), channel_id=1, replica_groups=mesh['y'=4,'x_lo'=2,'core'=2,'z_hi'=4,'z1'=2,'z0'=2,'x_hi'=2] {'y','x_lo..., dimensions={0} | all-to-all | bytes 524288 | tf_op jit(solution)/shard_map/all_to_all | solution.py:267
  49.2 10.3 %all_to_all.21.near_ref = f32[4,16,128]{2,1,0:T(8,128)S(1)} all-to-all(f32[4,16,128]{2,1,0:T(8,128)S(1)} %get-tuple-element.44), channel_id=1, replica_groups=mesh['y'=4,'x_lo'=2,'core'=2,'z_hi'=4,'z1'=2,'z0'=2,'x_hi'=2] {'z0','x_hi'}, dimensions={0} | all-to-all | bytes 65536 | tf_op jit(solution)/shard_map/all_to_all | solution.py:269
  59.5 0.0 collective-permute-done.4.far_ref
  59.5 0.6 shard_map.24
  60.1 10.9 %all_to_all.22.far_ref = f32[8,24,128]{2,1,0:T(8,128)S(1)} all-to-all(f32[8,24,128]{2,1,0:T(8,128)S(1)} %shard_map.24), channel_id=1, replica_groups=mesh['y'=4,'x_lo'=2,'core'=2,'z_hi'=4,'z1'=2,'z0'=2,'x_hi'=2] {'z1','x_l..., dimensions={0} | all-to-all | bytes 196608 | tf_op jit(solution)/shard_map/all_to_all | solution.py:271
  71.0 0.2 shard_map.25
  71.2 10.4 %all_to_all.23.shares_ref = f32[16,24,128]{2,1,0:T(8,128)S(1)} all-to-all(f32[16,24,128]{2,1,0:T(8,128)S(1)} %shard_map.25), channel_id=1, replica_groups=mesh['y'=4,'x_lo'=2,'core'=2,'z_hi'=4,'z1'=2,'z0'=2,'x_hi'=2] {'y','x_lo..., dimensions={0} | all-to-all | bytes 393216 | tf_op jit(solution)/shard_map/all_to_all | solution.py:272
  81.6 0.9 %shard_map.26 = f32[5,64,64]{2,1,0:T(8,128)} custom-call(f32[4,16,128]{2,1,0:T(8,128)S(1)} %all_to_all.21.near_ref, f32[8,24,128]{2,1,0:T(8,128)S(1)} %all_to_all.22.far_ref, f32[16,24,128]{2,1,0:T(8,128)S(1)} %all_to_all.23.shares_ref), custom_call_target="tpu_custom_call" | custom-call | tf_op jit(solution)/shard_map/pallas_call | solution.py:21
  (1 shorter events, 0.0 us)
Async XLA Ops:
  1.4 20.0 %collective-permute-start.3 = (f32[2,64,2048]{2,1,0:T(8,128)S(1)}, f32[2,64,2048]{2,1,0:T(8,128)S(1)}, u32[]{:S(2)}, u32[]{:S(2)}) collective-permute-start(f32[2,64,2048]{2,1,0:T(8,128)S(1)} %get-tuple-element.36), channel_id=1, source_target_pairs={{2,4},{4,2},{3,5},{5,3},{10,12},{12,10},{11,13},{13,11},{18,20},{2... | collective-permute-start | bytes 3145736 | tf_op jit(solution)/shard_map/ppermute | solution.py:249
  2.1 31.0 %collective-permute-start = (f32[2,64,1024]{2,1,0:T(8,128)S(1)}, f32[2,64,1024]{2,1,0:T(8,128)S(1)}, u32[]{:S(2)}, u32[]{:S(2)}) collective-permute-start(f32[2,64,1024]{2,1,0:T(8,128)S(1)} %get-tuple-element.27), channel_id=1, source_target_pairs={{0,3},{1,2},{2,1},{3,0},{4,7},{5,6},{6,5},{7,4},{8,11},{9,10},{10,... | collective-permute-start | bytes 1572872 | tf_op jit(solution)/shard_map/ppermute | solution.py:243
  13.0 22.4 %collective-permute-start.1 = (f32[2,64,1024]{2,1,0:T(8,128)S(1)}, f32[2,64,1024]{2,1,0:T(8,128)S(1)}, u32[]{:S(2)}, u32[]{:S(2)}) collective-permute-start(f32[2,64,1024]{2,1,0:T(8,128)S(1)} %get-tuple-element.34), channel_id=1, source_target_pairs={{0,1},{1,0},{2,3},{3,2},{4,5},{5,4},{6,7},{7,6},{8,9},{9,8},{10,11... | collective-permute-start | bytes 1572872 | tf_op jit(solution)/shard_map/ppermute | solution.py:243
  15.2 20.2 %collective-permute-start.2 = (f32[2,64,1024]{2,1,0:T(8,128)S(1)}, f32[2,64,1024]{2,1,0:T(8,128)S(1)}, u32[]{:S(2)}, u32[]{:S(2)}) collective-permute-start(f32[2,64,1024]{2,1,0:T(8,128)S(1)} %get-tuple-element.29), channel_id=1, source_target_pairs={{0,2},{1,3},{2,0},{3,1},{4,6},{5,7},{6,4},{7,5},{8,10},{9,11},{10,... | collective-permute-start | bytes 1572872 | tf_op jit(solution)/shard_map/ppermute | solution.py:243
  21.5 38.0 %collective-permute-start.4 = (f32[2,64,2048]{2,1,0:T(8,128)S(1)}, f32[2,64,2048]{2,1,0:T(8,128)S(1)}, u32[]{:S(2)}, u32[]{:S(2)}) collective-permute-start(f32[2,64,2048]{2,1,0:T(8,128)S(1)} %shard_map.21), channel_id=1, source_target_pairs={{0,4},{6,2},{4,6},{2,0},{1,5},{7,3},{5,7},{3,1},{8,12},{14,10},{12... | collective-permute-start | bytes 3145736 | tf_op jit(solution)/shard_map/ppermute | solution.py:261
